TPU v7x, 256 devices: a whole 4x4x8 slice. The times are simulated.
256 devices in a mesh: dp: 32 (over y, x, core), tp: 8 (over z).
Axes of the slice: x: 4, y: 4, z: 8, core: 2. Of those that a mesh axis runs over, the one named last changes fastest.
Arguments:
- cache_keys: bfloat16 [2048, 128, 256], P('dp', 'tp'), may hold values from -6 to 6
- cache_values: bfloat16 [2048, 128, 256], P('dp', 'tp'), may hold values from -6 to 6
- page_dest: int32 [2048, 1], P('dp'), may hold values from 0 to 31; in each aligned block of 64 rows (0 to 63, 64 to 127, ...) at most 4 rows name the same one
- lengths: int32 [128], P('dp'), may hold values from 1 to 2048, 87381 in all
- queries: bfloat16 [128, 4, 4096], P('dp'), may hold values from -128 to 128
- new_keys: bfloat16 [128, 4, 256], P('dp'), may hold values from -6 to 6
- new_values: bfloat16 [128, 4, 256], P('dp'), may hold values from -6 to 6
- residual: bfloat16 [128, 4, 4096], P('dp', None, 'tp'), may hold values from -4 to 4
- out_weight: bfloat16 [4096, 4096], P(None, 'tp'), may hold values from -1 to 1
- norm_gain: float32 [4096], P('tp'), may hold values from 0.5 to 2
- expert_ids: int32 [128, 4, 8], P('dp'), may hold values from 0 to 31, all different within a row; in each aligned block of 16 rows (0 to 15, 16 to 31, ..., all dimensions but the last counted through in order) at most 6 rows name the same one
- gate_probs: float32 [128, 4, 8], P('dp'), may hold values from 0.1 to 0.6
- w_gate: bfloat16 [32, 4096, 1536], P('dp', None, 'tp'), may hold values from -0.09375 to 0.09375
- w_up: bfloat16 [32, 4096, 1536], P('dp', None, 'tp'), may hold values from -0.09375 to 0.09375
- w_down: bfloat16 [32, 1536, 4096], P('dp', 'tp'), may hold values from -0.15625 to 0.15625
Outputs:
- moved_keys: bfloat16 [4096, 128, 256], P('dp', 'tp')
- moved_values: bfloat16 [4096, 128, 256], P('dp', 'tp')
- layer_out: bfloat16 [128, 4, 4096], P('dp', None, 'tp')
Inputs may be any that keep to these rules, and one draw needn't show every extreme that they name: `page_dest`: among the pages of one rank no rank is named more than 4 times. `expert_ids`: each token names 8 different experts; among the tokens of one rank no expert is named more than 6 times.
All inputs are finite; a program needn't handle non-finite values. No bound on the sum of `lengths` on one device may be relied on, other than what follows from the above.
Results may differ from a plain program's by a relative error of at most 0.02.
Values may be sent and summed in bfloat16 or wider, within the bound.
A program may use at most 64 MiB of HBM per device.

v0:
```python
import math

import jax
import jax.numpy as jnp
from jax import lax
from jax.sharding import PartitionSpec as P

QH = 32
KVH = 2
HEAD = 128
TOPK = 8


EPSILON = 1e-06


def merged(value, axis, join):
    pieces = jax.tree.map(lambda part: lax.all_gather(part, axis), value)
    head = jax.tree.map(lambda part: part[0], pieces)
    tail = jax.tree.map(lambda part: part[1:], pieces)
    subtotal, _ = lax.scan(lambda subtotal, slab: (join(subtotal, slab), None), head, tail)
    return subtotal


def slot_ranks(groups, count_to):
    onehot = (groups[..., None] == jnp.arange(count_to, dtype=jnp.int32)).astype(jnp.int32)
    before = jnp.cumsum(onehot, axis=1) - onehot
    return jnp.sum(before * onehot, axis=-1)


def join_softmax(earlier, later_one):
    top_score = jnp.maximum(earlier[0], later_one[0])
    early_scale = jnp.exp(earlier[0] - top_score)
    late_scale = jnp.exp(later_one[0] - top_score)
    weight_sum = earlier[1] * early_scale + later_one[1] * late_scale
    value_sum = earlier[2] * early_scale[..., None] + later_one[2] * late_scale[..., None]
    return (top_score, weight_sum, value_sum)


def shards(
    cache_keys,
    cache_values,
    page_dest,
    lengths,
    queries,
    new_keys,
    new_values,
    residual,
    out_weight,
    norm_gain,
    expert_ids,
    gate_probs,
    w_gate,
    w_up,
    w_down,
):
    dp_count = lax.axis_size("dp")
    slices = lax.axis_size("tp")
    part_index = lax.axis_index("tp")
    pages_local, slab_rows, kv_width = cache_keys.shape
    target = page_dest[:, 0]
    within = slot_ranks(target[None, :], dp_count)[0]
    cap_pages = (2 * pages_local + dp_count - 1) // dp_count
    outgoing_shape = (dp_count, cap_pages, slab_rows, kv_width)
    send_keys = jnp.zeros(outgoing_shape, jnp.bfloat16).at[target, within].set(cache_keys)
    send_values = jnp.zeros(outgoing_shape, jnp.bfloat16).at[target, within].set(cache_values)
    moved_keys, moved_values = (
        lax.all_to_all(send_keys, "dp", split_axis=0, concat_axis=0, tiled=True),
        lax.all_to_all(send_values, "dp", split_axis=0, concat_axis=0, tiled=True),
    )
    moved_keys = moved_keys.reshape(dp_count * cap_pages, slab_rows, kv_width)
    moved_values = moved_values.reshape(dp_count * cap_pages, slab_rows, kv_width)
    req_count, step_count, q_width = queries.shape
    group_size = QH // KVH
    pages_req = pages_local // req_count
    score_scale = 1.0 / math.sqrt(HEAD)
    local_keys = cache_keys.reshape(req_count, pages_req, slab_rows, KVH, HEAD)
    local_values = cache_values.reshape(req_count, pages_req, slab_rows, KVH, HEAD).astype(
        jnp.float32
    )
    page_number = jnp.arange(pages_req, dtype=jnp.int32)[:, None]
    row_number = jnp.arange(slab_rows, dtype=jnp.int32)[None, :]
    position = page_number * (slab_rows * slices) + part_index * slab_rows + row_number
    visible = (position[None, :, :] < lengths[:, None, None])[:, None, None, None, :, :]
    query_heads = queries.reshape(req_count, step_count, KVH, group_size, HEAD)
    scores = (
        jnp.einsum(
            "rskgd,rpjkd->rskgpj", query_heads, local_keys, preferred_element_type=jnp.float32
        )
        * score_scale
    )
    scores = jnp.where(visible, scores, -1e30)
    top_score = jnp.max(scores, axis=(-2, -1))
    weights = jnp.where(visible, jnp.exp(scores - top_score[..., None, None]), 0.0)
    weight_sum = jnp.sum(weights, axis=(-2, -1))
    value_sum = jnp.einsum(
        "rskgpj,rpjkd->rskgd", weights, local_values, precision=lax.Precision.HIGHEST
    )
    top_score, weight_sum, value_sum = merged(
        (top_score, weight_sum, value_sum), "tp", join_softmax
    )
    fresh_keys = new_keys.reshape(req_count, step_count, KVH, HEAD)
    fresh_values = new_values.reshape(req_count, step_count, KVH, HEAD).astype(jnp.float32)
    fresh_scores = (
        jnp.einsum("rskgd,rtkd->rskgt", query_heads, fresh_keys, preferred_element_type=jnp.float32)
        * score_scale
    )
    causal = (
        jnp.arange(step_count, dtype=jnp.int32)[:, None]
        >= jnp.arange(step_count, dtype=jnp.int32)[None, :]
    )
    causal = causal[None, :, None, None, :]
    fresh_scores = jnp.where(causal, fresh_scores, -1e30)
    best_score = jnp.maximum(top_score, jnp.max(fresh_scores, axis=-1))
    rescale = jnp.exp(top_score - best_score)
    fresh_weights = jnp.where(causal, jnp.exp(fresh_scores - best_score[..., None]), 0.0)
    weight_sum = weight_sum * rescale + jnp.sum(fresh_weights, axis=-1)
    value_sum = value_sum * rescale[..., None] + jnp.einsum(
        "rskgt,rtkd->rskgd", fresh_weights, fresh_values, precision=lax.Precision.HIGHEST
    )
    attended = (
        (value_sum / weight_sum[..., None])
        .reshape(req_count, step_count, q_width)
        .astype(jnp.bfloat16)
    )
    model_part = residual.shape[2]
    projected = jnp.dot(
        attended.reshape(-1, q_width), out_weight, preferred_element_type=jnp.float32
    )
    projected = projected.reshape(req_count, step_count, model_part)
    layer_state = (residual.astype(jnp.float32) + projected).astype(jnp.bfloat16)
    token_count = req_count * step_count
    flat_ids = expert_ids.reshape(1, -1)
    target_expert = flat_ids[0]
    within_expert = slot_ranks(flat_ids, dp_count)[0]
    slots_cap = min(token_count, (3 * token_count * TOPK + 2 * dp_count - 1) // (2 * dp_count))
    full_state, full_gain = (
        lax.all_gather(layer_state, "tp", axis=2, tiled=True),
        lax.all_gather(norm_gain.astype(jnp.bfloat16), "tp", axis=0, tiled=True).astype(
            norm_gain.dtype
        ),
    )
    state_wide = full_state.astype(jnp.float32)
    mean_square = jnp.mean(jnp.square(state_wide), axis=-1, keepdims=True)
    normed = (state_wide * lax.rsqrt(mean_square + EPSILON) * full_gain).astype(jnp.bfloat16)
    token_rows = jnp.repeat(normed.reshape(token_count, -1), TOPK, axis=0)
    outgoing = (
        jnp.zeros((dp_count, slots_cap, token_rows.shape[1]), jnp.bfloat16)
        .at[target_expert, within_expert]
        .set(token_rows)
    )
    arrived = lax.all_to_all(outgoing, "dp", split_axis=0, concat_axis=0, tiled=True)
    in_rows = arrived.reshape(-1, arrived.shape[2])
    gate_part = jnp.dot(in_rows, w_gate[0], preferred_element_type=jnp.float32)
    up_part = jnp.dot(in_rows, w_up[0], preferred_element_type=jnp.float32)
    hidden = (jax.nn.silu(gate_part) * up_part).astype(jnp.bfloat16)
    down_part = jnp.dot(hidden, w_down[0], preferred_element_type=jnp.float32)
    summed_part = lax.psum_scatter(down_part, "tp", scatter_dimension=1, tiled=True)
    finished = summed_part.astype(jnp.bfloat16).reshape(dp_count, slots_cap, -1)
    returned = lax.all_to_all(finished, "dp", split_axis=0, concat_axis=0, tiled=True)
    picked = (
        returned[target_expert, within_expert]
        .reshape(req_count, step_count, TOPK, -1)
        .astype(jnp.float32)
    )
    mixture = jnp.einsum("rsk,rskd->rsd", gate_probs, picked, precision=lax.Precision.HIGHEST)
    layer_out = (layer_state.astype(jnp.float32) + mixture).astype(jnp.bfloat16)
    return (moved_keys, moved_values, layer_out)


def solution(mesh):
    in_specs = (
        P("dp", "tp", None),
        P("dp", "tp", None),
        P("dp", None),
        P("dp"),
        P("dp", None, None),
        P("dp", None, None),
        P("dp", None, None),
        P("dp", None, "tp"),
        P(None, "tp"),
        P("tp"),
        P("dp", None, None),
        P("dp", None, None),
        P("dp", None, "tp"),
        P("dp", None, "tp"),
        P("dp", "tp", None),
    )
    out_specs = (P("dp", "tp", None), P("dp", "tp", None), P("dp", None, "tp"))
    return jax.shard_map(shards, mesh=mesh, in_specs=in_specs, out_specs=out_specs, check_vma=False)
```

profile of v0, /device:TPU:1, one launch (start us, length us, event | category | flops | bytes accessed | tf_op | source)
XLA Modules:
  0.0 290.7 jit_solution(5620240837521767560)
XLA Ops:
  7.3 1.2 reshape.347
  8.5 1.2 reshape.346
  9.6 1.2 reshape.348
  10.8 0.7 broadcast_compare_fusion
  11.5 1.1 bitcast_reduce_fusion
  12.6 4.2 %fusion.23 = f32[4,4,2,16,128]{4,3,1,2,0:T(8,128)S(1)} fusion(f32[4,2,16,16,4,16]{5,3,4,2,1,0:T(8,128)S(1)} %get-tuple-element.91, f32[4,4,2,16]{3,1,2,0:T(4,128)S(1)} %get-tuple-element.90, pred[4,16,16]{2,1,0:T(8,128)(4,1)S(1)} %broadcast_compare_fusion, bf16[4,16,16,2,128,1]{4,3,2,1,0,5:T(2,128)(2,1)S(1)} %bitcast.144), kind=kOutput, calls=%fused_computation.36 | convolution fusion | flops 201850880 | bytes 1313792 | tf_op jit(solution)/shard_map/rskgpj,rpjkd->rskgd/dot_general | solution.py:96
  16.9 0.7 copy.54
  17.7 3.0 %fusion.10 = f32[4,4,2,16]{3,1,2,0:T(4,128)S(1)} fusion(f32[4,2,16,16,4,16]{5,3,4,2,1,0:T(8,128)} %copy-done.1, f32[4,4,2,16]{3,1,2,0:T(4,128)S(1)} %get-tuple-element.90, pred[4,16,16]{2,1,0:T(8,128)(4,1)S(1)} %broadcast_compare_fusion), kind=kLoop, calls=%fused_computation.23 | loop fusion | flops 654848 | bytes 529408 | tf_op jit(solution)/shard_map/reduce_sum | solution.py:95
  20.7 24.4 %all-gather.1 = f32[32,4,2,16]{3,1,2,0:T(4,128)S(1)} all-gather(f32[4,4,2,16]{3,1,2,0:T(4,128)S(1)} %fusion.10), channel_id=3, replica_groups=mesh['dp'=32,'tp'=8] {'tp'}, dimensions={0}, use_global_device_ids=true | all-gather | bytes 18432 | tf_op jit(solution)/shard_map/all_gather | solution.py:18
  45.1 19.8 %all-gather = f32[32,4,2,16]{3,1,2,0:T(4,128)S(1)} all-gather(f32[4,4,2,16]{3,1,2,0:T(4,128)S(1)} %get-tuple-element.90), channel_id=2, replica_groups=mesh['dp'=32,'tp'=8] {'tp'}, dimensions={0}, use_global_device_ids=true | all-gather | bytes 18432 | tf_op jit(solution)/shard_map/all_gather | solution.py:18
  65.2 16.4 %all-gather.3 = bf16[8,1,512]{2,1,0:T(2,128)(2,1)S(1)} all-gather(bf16[1,1,512]{2,1,0:T(2,128)(2,1)S(1)} %reshape.392), channel_id=1, replica_groups=mesh['dp'=32,'tp'=8] {'tp'}, dimensions={0}, use_global_device_ids=true | all-gather | bytes 9216 | tf_op jit(solution)/shard_map/all_gather | solution.py:139
  82.6 3.0 %slice.43 = f32[28,4,2,16,128]{4,3,2,1,0:T(8,128)} slice(f32[32,4,2,16,128]{4,3,2,1,0:T(8,128)} %all-gather.6.cloned.1.call-done), slice={[4:32], [0:4], [0:2], [0:16], [0:128]} | slice | bytes 3670016 | tf_op jit(solution)/shard_map/slice | solution.py:20
  85.6 1.0 slice.40
  86.6 9.2 %while.14 = (s32[]{:T(128)}, f32[4,4,2,16]{3,2,1,0:T(2,128)S(1)}, f32[4,4,2,16]{3,2,1,0:T(2,128)S(1)}, f32[4,4,2,16,128]{4,3,2,1,0:T(8,128)S(1)}, f32[7,4,4,2,16...) while((s32[]{:T(128)}, f32[4,4,2,16]{3,2,1,0:T(2,128)S(1)}, ...), condition=%wide.region_7.8_spmd, body=%wide.region_6.7_spmd.sunk | while | flops 199682 | bytes 815197 | solution.py:21
  86.6 1.2 fusion.92
  87.9 1.2 fusion.92
  89.2 1.2 fusion.92
  90.6 1.2 fusion.92
  91.9 1.2 fusion.92
  93.2 1.2 fusion.92
  94.5 1.2 fusion.92
  95.9 0.5 fusion.28
  96.5 2.9 fusion.42
  99.4 18.2 %all_gather.30 = bf16[4,4,4096]{2,1,0:T(4,128)(2,1)S(1)} all-gather(bf16[4,4,512]{2,1,0:T(4,128)(2,1)S(1)} %fusion.42), channel_id=1, replica_groups=mesh['dp'=32,'tp'=8] {'tp'}, dimensions={2}, use_global_device_ids=true | all-gather | bytes 147456 | tf_op jit(solution)/shard_map/all_gather | solution.py:138
  118.0 1.1 broadcast_bitcast_fusion
  119.2 26.2 %scatter_fusion.2 = bf16[32,6,4096]{2,0,1:T(8,128)(2,1)S(1)} fusion(bf16[32,6,4096]{2,0,1:T(8,128)(2,1)S(1)} %broadcast_in_dim.79, s32[128]{0:T(128)S(1)} %get-tuple-element.86, bf16[128,4096]{1,0:T(8,128)(2,1)} %broadcast_bitcast_fusion), kind=kCustom, calls=%fused_computation.3 | custom fusion | bytes 3146752 | tf_op jit(solution)/shard_map/scatter | solution.py:150
  145.4 0.9 copy.67
  146.3 57.4 %all_to_all.20 = bf16[32,6,4096]{2,1,0:T(8,128)(2,1)} all-to-all(bf16[32,6,4096]{2,1,0:T(8,128)(2,1)S(1)} %copy.67), channel_id=1, replica_groups=mesh['dp'=32,'tp'=8] {'dp'}, dimensions={0} | all-to-all | bytes 3145728 | tf_op jit(solution)/shard_map/all_to_all | solution.py:152
  203.8 2.5 reshape.353
  206.3 2.1 fusion.21
  208.5 5.0 %fusion.17 = f32[192,4096]{1,0:T(8,128)} fusion(bf16[1,192,4096]{2,1,0:T(8,128)(2,1)S(1)} %copy-done, bf16[192,4096]{1,0:T(8,128)(2,1)S(1)} %reshape.353, bf16[1,4096,192]{1,2,0:T(8,128)(2,1)} %param.30, f32[192,192]{1,0:T(8,128)S(1)} %fusion.21), kind=kOutput, calls=%fused_computation.30 | convolution fusion | flops 604200960 | bytes 8011776 | tf_op jit(solution)/shard_map/dot_general | solution.py:157
  213.9 1.1 broadcast.231.clone
  214.9 7.3 %scatter_fusion = bf16[32,4,16,256]{3,2,1,0:T(8,128)(2,1)} fusion(bf16[32,4,16,256]{3,2,1,0:T(8,128)(2,1)} %broadcast.231.clone, s32[64]{0:T(128)S(1)} %fusion.72, bf16[64,16,256]{2,1,0:T(8,128)(2,1)S(1)} %copy-done.2), kind=kCustom, calls=%fused_computation.1 | custom fusion | bytes 1573376 | tf_op jit(solution)/shard_map/scatter | solution.py:65
  222.3 3.9 %all-to-all-start = ((bf16[32,4,16,256]{3,2,1,0:T(8,128)(2,1)}), bf16[32,4,16,256]{3,2,1,0:T(8,128)(2,1)S(1)}, u32[]{:S(2)}, u32[]{:S(2)}) async-start(bf16[32,4,16,256]{3,2,1,0:T(8,128)(2,1)} %scatter_fusion), calls=%async_computation | async-start | bytes 2097152 | tf_op jit(solution)/shard_map/all_to_all | solution.py:68
  226.2 1.1 broadcast.231.clone.1
  227.3 7.3 %scatter_fusion.1 = bf16[32,4,16,256]{3,2,1,0:T(8,128)(2,1)} fusion(bf16[32,4,16,256]{3,2,1,0:T(8,128)(2,1)} %broadcast.231.clone.1, s32[64]{0:T(128)S(1)} %fusion.72, bf16[64,16,256]{2,1,0:T(8,128)(2,1)S(1)} %copy-done.3), kind=kCustom, calls=%fused_computation.2 | custom fusion | bytes 1573376 | tf_op jit(solution)/shard_map/scatter | solution.py:66
  234.5 8.9 %all-to-all-done = bf16[32,4,16,256]{3,2,1,0:T(8,128)(2,1)S(1)} async-done(((bf16[32,4,16,256]{3,2,1,0:T(8,128)(2,1)}), bf16[32,4,16,256]{3,2,1,0:T(8,128)(2,1)S(1)}, u32[]{:S(2)}, u32[]{:S(2)}) %all-to-all-start) | async-done | bytes 1048608 | tf_op jit(solution)/shard_map/all_to_all | solution.py:68
  243.5 4.6 %all-to-all-start.1 = ((bf16[32,4,16,256]{3,2,1,0:T(8,128)(2,1)}), bf16[32,4,16,256]{3,2,1,0:T(8,128)(2,1)}, u32[]{:S(2)}, u32[]{:S(2)}) async-start(bf16[32,4,16,256]{3,2,1,0:T(8,128)(2,1)} %scatter_fusion.1), calls=%async_computation.1 | async-start | bytes 2097152 | tf_op jit(solution)/shard_map/all_to_all | solution.py:69
  248.1 4.1 %reduce-scatter.2.cloned.1.call-done = f32[192,512]{1,0:T(8,128)} async-done(((f32[192,4096]{1,0:T(8,128)}), f32[192,512]{1,0:T(8,128)}) %reduce-scatter.2.cloned.1.call-update) | async-done | bytes 393232 | tf_op jit(solution)/shard_map/reduce_scatter | solution.py:158
  252.2 1.0 convert_element_type.83
  253.2 0.8 reshape.354
  254.0 11.5 %all-to-all-done.1 = bf16[32,4,16,256]{3,2,1,0:T(8,128)(2,1)} async-done(((bf16[32,4,16,256]{3,2,1,0:T(8,128)(2,1)}), bf16[32,4,16,256]{3,2,1,0:T(8,128)(2,1)}, u32[]{:S(2)}, u32[]{:S(2)}) %all-to-all-start.1) | async-done | bytes 1048608 | tf_op jit(solution)/shard_map/all_to_all | solution.py:69
  265.5 3.9 %all-to-all-start.3 = ((bf16[32,6,512]{2,1,0:T(8,128)(2,1)}), bf16[32,6,512]{2,1,0:T(8,128)(2,1)S(1)}, u32[]{:S(2)}, u32[]{:S(2)}) async-start(bf16[32,6,512]{2,1,0:T(8,128)(2,1)} %reshape.354), calls=%async_computation.4 | async-start | bytes 524288 | tf_op jit(solution)/shard_map/all_to_all | solution.py:160
  269.4 9.0 %all-to-all-done.3 = bf16[32,6,512]{2,1,0:T(8,128)(2,1)S(1)} async-done(((bf16[32,6,512]{2,1,0:T(8,128)(2,1)}), bf16[32,6,512]{2,1,0:T(8,128)(2,1)S(1)}, u32[]{:S(2)}, u32[]{:S(2)}) %all-to-all-start.3) | async-done | bytes 196640 | tf_op jit(solution)/shard_map/all_to_all | solution.py:160
  278.5 1.3 gather_fusion
  280.0 0.6 fusion.62
  280.7 1.0 copy.146
  281.6 2.3 copy.147
  (76 shorter events, 3.2 us)
Async XLA Ops:
  7.2 201.3 %copy-start = (bf16[1,192,4096]{2,1,0:T(8,128)(2,1)S(1)}, bf16[1,192,4096]{2,1,0:T(8,128)(2,1)}, u32[]{:S(2)}) copy-start(bf16[1,192,4096]{2,1,0:T(8,128)(2,1)} %param.31) | copy-start | bytes 4718596
  7.2 75.4 %all-gather.6.cloned.1.call-start = ((), (), s32[]{:S(2)}) async-start(), calls=%async_computation.6 | async-start | bytes 2359296 | tf_op jit(solution)/shard_map/all_gather | solution.py:18
  12.6 4.2 %copy-start.1 = (f32[4,2,16,16,4,16]{5,3,4,2,1,0:T(8,128)}, f32[4,2,16,16,4,16]{5,3,4,2,1,0:T(8,128)S(1)}, u32[]{:S(2)}) copy-start(f32[4,2,16,16,4,16]{5,3,4,2,1,0:T(8,128)S(1)} %get-tuple-element.91) | copy-start | bytes 1572868
  16.9 48.1 %copy-start.4 = (s32[4,4,8]{2,1,0:T(4,128)S(1)}, s32[4,4,8]{2,1,0:T(4,128)}, u32[]{:S(2)}) copy-start(s32[4,4,8]{2,1,0:T(4,128)} %param.27) | copy-start | bytes 1540
  16.9 48.3 %copy-start.8 = (f32[512]{0:T(512)S(1)}, f32[512]{0:T(512)}, u32[]{:S(2)}) copy-start(f32[512]{0:T(512)} %param.26) | copy-start | bytes 6148
  16.9 65.2 %copy-start.9 = (bf16[4,4,256]{2,1,0:T(4,128)(2,1)S(1)}, bf16[4,4,256]{2,1,0:T(4,128)(2,1)}, u32[]{:S(2)}) copy-start(bf16[4,4,256]{2,1,0:T(4,128)(2,1)} %param.22) | copy-start | bytes 24580
  17.6 234.5 %reduce-scatter.2.cloned.1.call-start = ((), (), s32[]{:S(2)}) async-start(), calls=%async_computation.5 | async-start | bytes 3538944 | tf_op jit(solution)/shard_map/reduce_scatter | solution.py:158
  82.5 13.4 %copy-start.10 = (bf16[4,4,256]{2,1,0:T(4,128)(2,1)S(1)}, bf16[4,4,256]{2,1,0:T(4,128)(2,1)}, u32[]{:S(2)}) copy-start(bf16[4,4,256]{2,1,0:T(4,128)(2,1)} %param.23) | copy-start | bytes 24580
  85.6 10.9 %copy-start.5 = (bf16[4,4,512]{2,1,0:T(4,128)(2,1)S(1)}, bf16[4,4,512]{2,1,0:T(4,128)(2,1)}, u32[]{:S(2)}) copy-start(bf16[4,4,512]{2,1,0:T(4,128)(2,1)} %param.24) | copy-start | bytes 49156
  208.5 5.0 %copy-start.7 = (s32[64,1]{0,1:T(1,128)S(1)}, s32[64,1]{0,1:T(1,128)}, u32[]{:S(2)}) copy-start(s32[64,1]{0,1:T(1,128)} %param.19) | copy-start | bytes 772
  213.4 1.5 copy-start.2
  213.4 13.8 %copy-start.3 = (bf16[64,16,256]{2,1,0:T(8,128)(2,1)S(1)}, bf16[64,16,256]{2,1,0:T(8,128)(2,1)}, u32[]{:S(2)}) copy-start(bf16[64,16,256]{2,1,0:T(8,128)(2,1)} %param.18) | copy-start | bytes 1572868
  222.3 21.2 %all-to-all-start = ((bf16[32,4,16,256]{3,2,1,0:T(8,128)(2,1)}), bf16[32,4,16,256]{3,2,1,0:T(8,128)(2,1)S(1)}, u32[]{:S(2)}, u32[]{:S(2)}) async-start(bf16[32,4,16,256]{3,2,1,0:T(8,128)(2,1)} %scatter_fusion), calls=%async_computation | async-start | bytes 2097152 | tf_op jit(solution)/shard_map/all_to_all | solution.py:68
  226.2 53.6 %copy-start.6 = (f32[4,4,8]{2,1,0:T(4,128)S(1)}, f32[4,4,8]{2,1,0:T(4,128)}, u32[]{:S(2)}) copy-start(f32[4,4,8]{2,1,0:T(4,128)} %param.28) | copy-start | bytes 1540
  243.5 22.0 %all-to-all-start.1 = ((bf16[32,4,16,256]{3,2,1,0:T(8,128)(2,1)}), bf16[32,4,16,256]{3,2,1,0:T(8,128)(2,1)}, u32[]{:S(2)}, u32[]{:S(2)}) async-start(bf16[32,4,16,256]{3,2,1,0:T(8,128)(2,1)} %scatter_fusion.1), calls=%async_computation.1 | async-start | bytes 2097152 | tf_op jit(solution)/shard_map/all_to_all | solution.py:69
  265.5 12.9 %all-to-all-start.3 = ((bf16[32,6,512]{2,1,0:T(8,128)(2,1)}), bf16[32,6,512]{2,1,0:T(8,128)(2,1)S(1)}, u32[]{:S(2)}, u32[]{:S(2)}) async-start(bf16[32,6,512]{2,1,0:T(8,128)(2,1)} %reshape.354), calls=%async_computation.4 | async-start | bytes 524288 | tf_op jit(solution)/shard_map/all_to_all | solution.py:160
Sparse Core Ops, SparseCore 0:
  17.8 42.1 all-gather.5
  213.6 38.5 reduce-scatter.1
where the time goes:
time: 292 us; the launch traced here: 291 us
  blocking collectives  136 us (47%)
  local copies, waits for them, and re-layouts  61.6 us (21%)
  waiting for transfers between devices  33.5 us (11%)
  matrix products  16.5 us (6%)
  other arithmetic  15.6 us (5%)
  between operations  14.5 us (5%)
  starting transfers between devices  12.5 us (4%)
    all_to_all x1, blocking collectives, shards(): lax.all_to_all(outgoing, 'dp', split_axis=0, concat_axis=0, tiled=True)  57.4 us
    all_gather x2, blocking collectives, merged(): pieces = jax.tree.map(lambda part: lax.all_gather(part, axis), value)  44.2 us
    scatter x2, local copies, waits for them, and re-layouts, shards(): outgoing = jnp.zeros((dp_count, slots_cap, token_rows.shape[1]), jnp.bflo...  27.1 us
    all_gather x1, blocking collectives, shards(): lax.all_gather(layer_state, 'tp', axis=2, tiled=True)  18.2 us
    all_gather x1, blocking collectives, shards(): lax.all_gather(norm_gain.astype(jnp.bfloat16), 'tp', axis=0, tiled=True)  16.4 us
    all_to_all x1, waiting for transfers between devices, shards(): lax.all_to_all(send_values, 'dp', split_axis=0, concat_axis=0, tiled=True)  11.5 us
    all_to_all x1, waiting for transfers between devices, shards(): lax.all_to_all(finished, 'dp', split_axis=0, concat_axis=0, tiled=True)  9.01 us
    all_to_all x1, waiting for transfers between devices, shards(): lax.all_to_all(send_keys, 'dp', split_axis=0, concat_axis=0, tiled=True)  8.92 us
  transfers between devices with their start and end apart: 5, of which 4 were waited for; matrix products, arithmetic and copies ran while one was open for 8% of the time, Pallas kernels for 0%

commit v1 on v0

v1 whole, which is shorter than its diff:
```python
import math

import jax
import jax.numpy as jnp
from jax import lax
from jax.experimental import pallas as pl
from jax.experimental.pallas import tpu as pltpu
from jax.sharding import PartitionSpec as P

MESH = pl.DeviceIdType.MESH
F32 = jnp.float32
BF16 = jnp.bfloat16

DP = 32
TP = 8
HEAD = 128
TOKENS = 16
SLOTS = 6
PAD_SLOTS = 8
ROWS = DP * SLOTS
HALF = ROWS // 2
PART = 512
WIDE = 256
BLOCK = 16
EPSILON = 1e-06
LOW = -1e30


def iota(shape, dim):
    return lax.broadcasted_iota(jnp.int32, shape, dim)


def onehot(mask):
    return jnp.where(mask, 1.0, 0.0).astype(BF16)


def dot(a, b):
    return jnp.dot(a, b, preferred_element_type=F32)


def dot_last(a, b):
    return lax.dot_general(a, b, (((1,), (1,)), ((), ())), preferred_element_type=F32)


def split_three(value):
    top = value.astype(BF16).astype(F32)
    rest = value - top
    middle = rest.astype(BF16).astype(F32)
    return top, middle, rest - middle


def layer_kernel(
    inverse, lengths, queries, new_keys, new_values, residual, gain, scatter, gather,
    keys, values, out_weight, w_gate, w_up, w_down,
    moved_keys, moved_values, layer_out,
    kbuf, vbuf, ksend, vsend, wo, wg, wu, wd,
    part_send, part_recv, coeff, attended, state,
    disp_send, disp_recv, xbuf, sqbuf, gate_acc, up_acc, ybuf,
    lsend, rsend, lrecv, rrecv, ret_send, ret_recv,
    local_sem, page_send_sem, page_recv_sem, part_ssem, part_rsem, att_ssem, att_rsem,
    disp_ssem, disp_rsem, sq_ssem, sq_rsem, ring_ssem, ring_rsem, red_ssem, red_rsem,
    ret_ssem, ret_rsem,
):
    me = lax.axis_index("dp")
    t = lax.axis_index("tp")

    def local(src, dst, i):
        return pltpu.make_async_copy(src, dst, local_sem.at[i])

    loads = [
        local(keys, kbuf.at[pl.ds(0, 64)], 0),
        local(values, vbuf.at[pl.ds(0, 64)], 1),
        local(out_weight, wo, 2),
        local(w_gate, wg, 3),
        local(w_up, wu, 4),
        local(w_down, wd, 5),
    ]
    for load in loads:
        load.start()

    barrier = pltpu.get_barrier_semaphore()

    @pl.loop(1, DP)
    def _(d):
        pl.semaphore_signal(
            barrier, inc=1, device_id=(lax.rem(me + d, DP), t), device_id_type=MESH
        )

    for d in range(1, TP):
        pl.semaphore_signal(
            barrier, inc=1, device_id=(me, lax.rem(t + d, TP)), device_id_type=MESH
        )

    kbuf[64] = jnp.zeros((16, WIDE), BF16)
    vbuf[64] = jnp.zeros((16, WIDE), BF16)
    loads[0].wait()
    loads[1].wait()

    row = iota((256, 256), 0)
    col = iota((256, 256), 1)
    perm = onehot(col == ((row >> 2) & 15) * 16 + (row >> 6) * 4 + (row & 3))
    perm_back = onehot(col == ((row >> 2) & 3) * 64 + (row >> 4) * 4 + (row & 3))
    scale = 1.0 / math.sqrt(HEAD)
    lane = iota((64, 256), 1)
    position = (lane >> 4) * 128 + t * 16 + (lane & 15)
    frow = iota((64, TOKENS), 0)
    fcol = iota((64, TOKENS), 1)
    stat_lane = iota((256, HEAD), 1)
    for k in range(2):
        cols = slice(k * HEAD, (k + 1) * HEAD)
        q_rows = jnp.concatenate(
            [queries[:, (k * 16 + g) * HEAD : (k * 16 + g + 1) * HEAD] for g in range(16)], axis=0
        )
        q_rows = dot(perm, q_rows).astype(BF16)
        fresh_k = new_keys[:, cols]
        fresh_v = new_values[:, cols]
        accs, tops, sums = [], [], []
        for r in range(4):
            k_r = kbuf[16 * r : 16 * r + 16].reshape(256, WIDE)[:, cols]
            v_r = vbuf[16 * r : 16 * r + 16].reshape(256, WIDE)[:, cols]
            q_r = q_rows[64 * r : 64 * r + 64]
            visible = position < lengths[r]
            scores = jnp.where(visible, dot_last(q_r, k_r) * scale, LOW)
            fvisible = ((fcol >> 2) == r) & ((fcol & 3) <= (frow & 3)) & (t == 0)
            fscores = jnp.where(fvisible, dot_last(q_r, fresh_k) * scale, LOW)
            top = jnp.maximum(
                jnp.max(scores, axis=1, keepdims=True), jnp.max(fscores, axis=1, keepdims=True)
            )
            weights = jnp.where(visible, jnp.exp(scores - top), 0.0)
            fweights = jnp.where(fvisible, jnp.exp(fscores - top), 0.0)
            sums.append(
                jnp.sum(weights, axis=1, keepdims=True) + jnp.sum(fweights, axis=1, keepdims=True)
            )
            tops.append(top)
            accs.append(dot(weights.astype(BF16), v_r) + dot(fweights.astype(BF16), fresh_v))
        acc = dot(perm_back, jnp.concatenate(accs, axis=0).astype(BF16)).astype(BF16)
        stats = jnp.zeros((256, HEAD), F32)
        pieces = split_three(jnp.concatenate(tops, axis=0)) + split_three(
            jnp.concatenate(sums, axis=0)
        )
        for i, piece in enumerate(pieces):
            stats = jnp.where(stat_lane == i, piece, stats)
        stats = jnp.transpose(stats)[0:16].astype(BF16)
        stats = dot(stats, perm).astype(BF16)
        for q in range(4):
            part_send[k * 4 + q, 0:64] = acc[64 * q : 64 * q + 64]
            part_send[k * 4 + q, 64:80] = stats[:, 128 * (q >> 1) : 128 * (q >> 1) + 128]

    pl.semaphore_wait(barrier, DP - 1 + TP - 1)

    def part_copy(d):
        dest = lax.rem(t + d, TP)
        return pltpu.make_async_remote_copy(
            src_ref=part_send.at[dest],
            dst_ref=part_recv.at[t],
            send_sem=part_ssem.at[d],
            recv_sem=part_rsem.at[t],
            device_id=(me, dest),
            device_id_type=MESH,
        )

    for d in range(1, TP):
        part_copy(d).start()
    part_recv[t] = part_send[t]

    @pl.loop(0, 128)
    def _(slot):
        page = inverse[slot]
        ksend[slot] = kbuf[page]
        vsend[slot] = vbuf[page]

    def page_copy(which, d):
        dest = lax.rem(me + d, DP)
        src, dst = ((ksend, moved_keys), (vsend, moved_values))[which]
        return pltpu.make_async_remote_copy(
            src_ref=src.at[pl.ds(dest * 4, 4)],
            dst_ref=dst.at[pl.ds(me * 4, 4)],
            send_sem=page_send_sem.at[which, dest],
            recv_sem=page_recv_sem.at[which, me],
            device_id=(dest, t),
            device_id_type=MESH,
        )

    @pl.loop(1, DP)
    def _(d):
        page_copy(0, d).start()
        page_copy(1, d).start()

    own_k = local(ksend.at[pl.ds(me * 4, 4)], moved_keys.at[pl.ds(me * 4, 4)], 6)
    own_v = local(vsend.at[pl.ds(me * 4, 4)], moved_values.at[pl.ds(me * 4, 4)], 7)
    own_k.start()
    own_v.start()

    def wait_recv(ref, sem):
        pltpu.make_async_copy(ref, ref, sem).wait()

    for d in range(1, TP):
        src = lax.rem(t + d, TP)
        wait_recv(part_recv.at[src], part_rsem.at[src])
    tops, sums = [], []
    for s in range(TP):
        stat = part_recv[s, 64:80].astype(F32)
        tops.append(stat[0:1] + stat[1:2] + stat[2:3])
        sums.append(stat[3:4] + stat[4:5] + stat[5:6])
    tops = jnp.concatenate(tops, axis=0)
    sums = jnp.concatenate(sums, axis=0)
    scales = jnp.exp(tops - jnp.max(tops, axis=0, keepdims=True))
    scales = scales / jnp.sum(scales * sums, axis=0, keepdims=True)
    scales = jnp.concatenate([scales, jnp.zeros((120, HEAD), F32)], axis=0)
    coeff[...] = jnp.transpose(scales)
    mine = coeff[pl.ds(pl.multiple_of((t & 1) * 64, 64), 64), :]
    merged = jnp.zeros((64, HEAD), F32)
    for s in range(TP):
        merged = merged + mine[:, s : s + 1] * part_recv[s, 0:64].astype(F32)
    merged = merged.astype(BF16)
    for h in range(4):
        attended[t, :, h * HEAD : (h + 1) * HEAD] = merged[h * 16 : h * 16 + 16]

    def att_copy(d):
        return pltpu.make_async_remote_copy(
            src_ref=attended.at[t],
            dst_ref=attended.at[t],
            send_sem=att_ssem.at[d],
            recv_sem=att_rsem.at[t],
            device_id=(me, lax.rem(t + d, TP)),
            device_id_type=MESH,
        )

    for d in range(1, TP):
        att_copy(d).start()

    loads[2].wait()

    def project(src):
        return dot(attended[src], wo[pl.ds(pl.multiple_of(src * PART, PART), PART), :])

    projected = project(t)
    for d in (1, 7, 2, 6, 3, 5, 4):
        src = lax.rem(t + d, TP)
        wait_recv(attended.at[src], att_rsem.at[src])
        projected = projected + project(src)
    layer_state = (residual[...].astype(F32) + projected).astype(BF16)
    state[...] = layer_state

    stacked = jnp.concatenate([layer_state[:, :WIDE], layer_state[:, WIDE:]], axis=0)
    disp_send[...] = dot(scatter[...], stacked).astype(BF16)

    def block_of(ref, rank):
        return ref.at[pl.ds(pl.multiple_of(rank * BLOCK, BLOCK), BLOCK)]

    def all_copy(send, recv, ssem, rsem, d):
        dest = lax.rem(me + d, DP)
        return pltpu.make_async_remote_copy(
            src_ref=block_of(send, dest),
            dst_ref=block_of(recv, me),
            send_sem=ssem.at[dest],
            recv_sem=rsem.at[me],
            device_id=(dest, t),
            device_id_type=MESH,
        )

    def exchange(send, recv, ssem, rsem):
        @pl.loop(1, DP)
        def _(d):
            all_copy(send, recv, ssem, rsem, d).start()

        block = pl.ds(pl.multiple_of(me * BLOCK, BLOCK), BLOCK)
        recv[block, :] = send[block, :]

        @pl.loop(1, DP)
        def _(d):
            src = lax.rem(me + d, DP)
            wait_recv(block_of(recv, src), rsem.at[src])

    exchange(disp_send, disp_recv, disp_ssem, disp_rsem)

    prow = iota((ROWS, DP * BLOCK), 0)
    pcol = iota((ROWS, DP * BLOCK), 1)
    place = (prow & 31) * BLOCK + (prow >> 5)
    arrived = disp_recv[...]
    square = jnp.zeros((ROWS, 1), F32)
    for h in range(2):
        piece = dot(onehot(pcol == place + h * PAD_SLOTS), arrived)
        square = square + jnp.sum(piece * piece, axis=1, keepdims=True)
        xbuf[t, :, h * WIDE : (h + 1) * WIDE] = (
            piece * gain[:, h * WIDE : (h + 1) * WIDE]
        ).astype(BF16)
    square = jnp.concatenate([square, jnp.zeros((256 - ROWS, 1), F32)], axis=0)
    sqbuf[t] = jnp.transpose(jnp.broadcast_to(square, (256, HEAD)))[0:1]

    def sq_copy(d):
        return pltpu.make_async_remote_copy(
            src_ref=sqbuf.at[t],
            dst_ref=sqbuf.at[t],
            send_sem=sq_ssem.at[d],
            recv_sem=sq_rsem.at[t],
            device_id=(me, lax.rem(t + d, TP)),
            device_id_type=MESH,
        )

    for d in range(1, TP):
        sq_copy(d).start()

    toward = (lax.rem(t + 1, TP), lax.rem(t + TP - 1, TP))

    def rows_of(sub):
        return pl.ds(sub * HALF, HALF)

    def ring_copy(way, i):
        step = i // 2
        chunk = lax.rem(t + (TP - step if way == 0 else step), TP)
        piece = xbuf.at[chunk, rows_of((i + way) % 2)]
        return pltpu.make_async_remote_copy(
            src_ref=piece,
            dst_ref=piece,
            send_sem=ring_ssem.at[way, i],
            recv_sem=ring_rsem.at[way, i],
            device_id=(me, toward[way]),
            device_id_type=MESH,
        )

    def ring_wait(way, i):
        step = i // 2 + 1
        chunk = lax.rem(t + (TP - step if way == 0 else step), TP)
        wait_recv(xbuf.at[chunk, rows_of((i + way) % 2)], ring_rsem.at[way, i])

    def expert_in(chunk, first=False):
        x = xbuf[chunk]
        weight_rows = pl.ds(pl.multiple_of(chunk * PART, PART), PART)
        gate_part = dot(x, wg[weight_rows, :])
        up_part = dot(x, wu[weight_rows, :])
        if first:
            gate_acc[...] = gate_part
            up_acc[...] = up_part
        else:
            gate_acc[...] += gate_part
            up_acc[...] += up_part

    for i in range(2):
        for way in range(2):
            ring_copy(way, i).start()
    loads[3].wait()
    loads[4].wait()
    expert_in(t, first=True)
    for i in range(7):
        for way in range(2):
            ring_wait(way, i)
            if i + 2 < 7:
                ring_copy(way, i + 2).start()
        if i % 2 == 1:
            expert_in(lax.rem(t + TP - (i // 2 + 1), TP))
            expert_in(lax.rem(t + i // 2 + 1, TP))
    expert_in(lax.rem(t + 4, TP))

    for d in range(1, TP):
        src = lax.rem(t + d, TP)
        wait_recv(sqbuf.at[src], sq_rsem.at[src])
    total = sqbuf[0]
    for s in range(1, TP):
        total = total + sqbuf[s]
    inv_norm = lax.rsqrt(total * (1.0 / (TP * PART)) + EPSILON)
    inv_norm = jnp.transpose(jnp.broadcast_to(inv_norm, (HEAD, 256)))[0:ROWS, 0:1]
    gate_part = gate_acc[...] * inv_norm
    up_part = up_acc[...] * inv_norm
    hidden = (gate_part / (1.0 + jnp.exp(-gate_part)) * up_part).astype(BF16)

    loads[5].wait()
    sends = (rsend, lsend)
    recvs = (rrecv, lrecv)

    def expert_out(chunk):
        ybuf[chunk] = dot(hidden, wd[:, pl.ds(pl.multiple_of(chunk * PART, PART), PART)])

    def red_copy(way, j):
        return pltpu.make_async_remote_copy(
            src_ref=sends[way].at[j],
            dst_ref=recvs[way].at[j],
            send_sem=red_ssem.at[way, j],
            recv_sem=red_rsem.at[way, j],
            device_id=(me, toward[way]),
            device_id_type=MESH,
        )

    for j in range(7):
        for way in range(2):
            distance = 4 - (j + 1) // 2
            chunk = lax.rem(t + (distance if way == 0 else TP - distance), TP)
            sub = (j + 1 + way) % 2
            if j == 0:
                if way == 0:
                    expert_out(chunk)
            elif j % 2 == 1:
                expert_out(chunk)
            value = ybuf[chunk, sub * HALF : (sub + 1) * HALF]
            if j >= 2:
                wait_recv(recvs[way].at[j - 2], red_rsem.at[way, j - 2])
                value = value + recvs[way][j - 2].astype(F32)
            sends[way][j] = value.astype(BF16)
            red_copy(way, j).start()
    expert_out(t)
    for j in (5, 6):
        for way in range(2):
            wait_recv(recvs[way].at[j], red_rsem.at[way, j])
    results = []
    for sub in range(2):
        value = ybuf[t, sub * HALF : (sub + 1) * HALF]
        value = value + recvs[0][5 + sub].astype(F32)
        value = value + recvs[1][6 - sub].astype(F32)
        results.append(value.astype(BF16))
    result = jnp.concatenate(results, axis=0)

    rrow = iota((DP * BLOCK, ROWS), 0)
    rcol = iota((DP * BLOCK, ROWS), 1)
    rplace = (rrow & 7) * DP + (rrow >> 4)
    back = jnp.zeros((DP * BLOCK, WIDE), F32)
    for h in range(2):
        pick = onehot((rcol == rplace) & (((rrow >> 3) & 1) == h))
        back = back + dot(pick, result[:, h * WIDE : (h + 1) * WIDE])
    ret_send[...] = back.astype(BF16)
    exchange(ret_send, ret_recv, ret_ssem, ret_rsem)

    weights = gather[...]
    weights_top = weights.astype(BF16)
    weights_rest = (weights - weights_top.astype(F32)).astype(BF16)
    returned = ret_recv[...]
    mixture = dot(weights_top, returned) + dot(weights_rest, returned)
    for h in range(2):
        features = slice(h * WIDE, (h + 1) * WIDE)
        layer_out[:, features] = (
            state[:, features].astype(F32) + mixture[h * TOKENS : (h + 1) * TOKENS]
        ).astype(BF16)

    own_k.wait()
    own_v.wait()

    @pl.loop(1, DP)
    def _(d):
        src = lax.rem(me + d, DP)
        dst = pl.ds(src * 4, 4)
        wait_recv(moved_keys.at[dst], page_recv_sem.at[0, src])
        wait_recv(moved_values.at[dst], page_recv_sem.at[1, src])
        page_copy(0, d).wait_send()
        page_copy(1, d).wait_send()
        all_copy(disp_send, disp_recv, disp_ssem, disp_rsem, d).wait_send()
        all_copy(ret_send, ret_recv, ret_ssem, ret_rsem, d).wait_send()

    for d in range(1, TP):
        part_copy(d).wait_send()
        att_copy(d).wait_send()
        sq_copy(d).wait_send()
    for i in range(7):
        for way in range(2):
            ring_copy(way, i).wait_send()
            red_copy(way, i).wait_send()


def layer(inverse, lengths, queries, new_keys, new_values, residual, gain, scatter, gather,
          keys, values, out_weight, w_gate, w_up, w_down):
    smem = pl.BlockSpec(memory_space=pltpu.SMEM)
    vmem = pl.BlockSpec(memory_space=pltpu.VMEM)
    hbm = pl.BlockSpec(memory_space=pl.ANY)
    dma = pltpu.SemaphoreType.DMA
    return pl.pallas_call(
        layer_kernel,
        out_shape=(
            jax.ShapeDtypeStruct((128, 16, WIDE), BF16),
            jax.ShapeDtypeStruct((128, 16, WIDE), BF16),
            jax.ShapeDtypeStruct((TOKENS, PART), BF16),
        ),
        in_specs=[smem, smem] + [vmem] * 7 + [hbm] * 6,
        out_specs=(hbm, hbm, vmem),
        scratch_shapes=[
            pltpu.VMEM((65, 16, WIDE), BF16),
            pltpu.VMEM((65, 16, WIDE), BF16),
            pltpu.VMEM((128, 16, WIDE), BF16),
            pltpu.VMEM((128, 16, WIDE), BF16),
            pltpu.VMEM((4096, PART), BF16),
            pltpu.VMEM((4096, 192), BF16),
            pltpu.VMEM((4096, 192), BF16),
            pltpu.VMEM((192, 4096), BF16),
            pltpu.VMEM((TP, 80, HEAD), BF16),
            pltpu.VMEM((TP, 80, HEAD), BF16),
            pltpu.VMEM((HEAD, HEAD), F32),
            pltpu.VMEM((TP, TOKENS, PART), BF16),
            pltpu.VMEM((TOKENS, PART), BF16),
            pltpu.VMEM((DP * BLOCK, WIDE), BF16),
            pltpu.VMEM((DP * BLOCK, WIDE), BF16),
            pltpu.VMEM((TP, ROWS, PART), BF16),
            pltpu.VMEM((TP, 1, 256), F32),
            pltpu.VMEM((ROWS, 192), F32),
            pltpu.VMEM((ROWS, 192), F32),
            pltpu.VMEM((TP, ROWS, PART), F32),
            pltpu.VMEM((7, HALF, PART), BF16),
            pltpu.VMEM((7, HALF, PART), BF16),
            pltpu.VMEM((7, HALF, PART), BF16),
            pltpu.VMEM((7, HALF, PART), BF16),
            pltpu.VMEM((DP * BLOCK, WIDE), BF16),
            pltpu.VMEM((DP * BLOCK, WIDE), BF16),
            dma((8,)),
            dma((2, DP)), dma((2, DP)),
            dma((TP,)), dma((TP,)), dma((TP,)), dma((TP,)),
            dma((DP,)), dma((DP,)),
            dma((TP,)), dma((TP,)),
            dma((2, 7)), dma((2, 7)), dma((2, 7)), dma((2, 7)),
            dma((DP,)), dma((DP,)),
        ],
        compiler_params=pltpu.CompilerParams(
            collective_id=0, has_side_effects=True, vmem_limit_bytes=48 * 1024 * 1024
        ),
    )(inverse, lengths, queries, new_keys, new_values, residual, gain, scatter, gather,
      keys, values, out_weight, w_gate, w_up, w_down)


def shards(
    cache_keys, cache_values, page_dest, lengths, queries, new_keys, new_values, residual,
    out_weight, norm_gain, expert_ids, gate_probs, w_gate, w_up, w_down,
):
    target = page_dest[:, 0]
    number = jnp.arange(64, dtype=jnp.int32)
    earlier = (target[:, None] == target[None, :]) & (number[None, :] < number[:, None])
    within = jnp.sum(earlier.astype(jnp.int32), axis=1)
    slot = target * 4 + within
    hit = slot[None, :] == jnp.arange(128, dtype=jnp.int32)[:, None]
    inverse = 64 + jnp.sum(jnp.where(hit, number[None, :] - 64, 0), axis=1)

    ids = expert_ids.reshape(TOKENS, -1)
    probs = gate_probs.reshape(TOKENS, -1)
    named = ids[:, :, None] == jnp.arange(DP, dtype=jnp.int32)
    member = jnp.any(named, axis=1)
    weight = jnp.sum(jnp.where(named, probs[:, :, None], 0.0), axis=1)
    token = jnp.arange(TOKENS, dtype=jnp.int32)
    before = jnp.where(token[None, :] < token[:, None], 1, 0)
    rank = jnp.sum(before[:, :, None] * member.astype(jnp.int32)[None], axis=1)
    slots = jnp.arange(PAD_SLOTS, dtype=jnp.int32)
    chosen = (member[:, :, None] & (rank[:, :, None] == slots)).astype(F32)
    halves = jnp.eye(2, dtype=F32)
    scatter = (
        chosen.transpose(1, 2, 0)[:, None, :, None, :] * halves[None, :, None, :, None]
    ).reshape(DP * BLOCK, 2 * TOKENS).astype(BF16)
    gather = (
        (chosen * weight[:, :, None])[None, :, :, None, :] * halves[:, None, None, :, None]
    ).reshape(2 * TOKENS, DP * BLOCK)

    moved_keys, moved_values, layer_out = layer(
        inverse,
        lengths,
        queries.reshape(TOKENS, -1),
        new_keys.reshape(TOKENS, -1),
        new_values.reshape(TOKENS, -1),
        residual.reshape(TOKENS, -1),
        norm_gain[None, :],
        scatter,
        gather,
        cache_keys,
        cache_values,
        out_weight,
        w_gate[0],
        w_up[0],
        w_down[0],
    )
    return moved_keys, moved_values, layer_out.reshape(residual.shape)


def solution(mesh):
    in_specs = (
        P("dp", "tp", None),
        P("dp", "tp", None),
        P("dp", None),
        P("dp"),
        P("dp", None, None),
        P("dp", None, None),
        P("dp", None, None),
        P("dp", None, "tp"),
        P(None, "tp"),
        P("tp"),
        P("dp", None, None),
        P("dp", None, None),
        P("dp", None, "tp"),
        P("dp", None, "tp"),
        P("dp", "tp", None),
    )
    out_specs = (P("dp", "tp", None), P("dp", "tp", None), P("dp", None, "tp"))
    return jax.shard_map(shards, mesh=mesh, in_specs=in_specs, out_specs=out_specs, check_vma=False)
```

time: 292 us -> 118 us (0.40)
  blocking collectives: 136 us -> 0 us
  Pallas kernels: 0 us -> 96.1 us
  local copies, waits for them, and re-layouts: 61.6 us -> 16.5 us
  waiting for transfers between devices: 33.5 us -> 0 us
  matrix products: 16.5 us -> 0 us
  between operations: 14.5 us -> 0.77 us
  starting transfers between devices: 12.5 us -> 0 us
  other arithmetic: 15.6 us -> 4.08 us
    pallas_call x0 -> x1, Pallas kernels: none -> 96.1 us  [layer(): pl.pallas_call(layer_kernel, out_shape=(jax.ShapeDtypeStruct((128, 16, WI...]
    all_gather x4 -> x0, blocking collectives: 78.8 us -> none  [the longest x2 44.2 us: merged(): pieces = jax.tree.map(lambda part: lax.all_gather(part, axis), value)]
    all_to_all x1 -> x0, blocking collectives: 57.4 us -> none  [shards(): lax.all_to_all(outgoing, 'dp', split_axis=0, concat_axis=0, tiled=True)]
    scatter x4 -> x0, local copies, waits for them, and re-layouts: 41.6 us -> none  [the longest x2 27.1 us: shards(): outgoing = jnp.zeros((dp_count, slots_cap, token_rows.shape[1]), jnp.bflo...]
    all_to_all x3 -> x0, waiting for transfers between devices: 29.4 us -> none  [the longest x1 11.5 us: shards(): lax.all_to_all(send_values, 'dp', split_axis=0, concat_axis=0, tiled=True)]
    dot_general x8 -> x0, matrix products: 16.5 us -> none  [the longest x1 4.95 us: shards(): down_part = jnp.dot(hidden, w_down[0], preferred_element_type=jnp.float32)]
    all_to_all x3 -> x0, starting transfers between devices: 12.5 us -> none  [the longest x1 4.64 us: shards(): lax.all_to_all(send_values, 'dp', split_axis=0, concat_axis=0, tiled=True)]
    add x17 -> x1, other arithmetic: 9 us -> 0.01 us  [shards(): inverse = 64 + jnp.sum(jnp.where(hit, number[None, :] - 64, 0), axis=1)]
  transfers between devices with their start and end apart: 5 -> 0, of which waited for: 4 -> 0; matrix products, arithmetic and copies ran while one was open for 8% -> 0% of each run, Pallas kernels for 0% -> 0%
where the time goes in v1:
time: 118 us; the launch traced here: 117 us
  Pallas kernels  96.1 us (81%)
  local copies, waits for them, and re-layouts  16.5 us (14%)
  other arithmetic  4.08 us (3%)
    pallas_call x1, Pallas kernels, layer(): pl.pallas_call(layer_kernel, out_shape=(jax.ShapeDtypeStruct((128, 16, WI...  96.1 us
    unnamed x18, local copies, waits for them, and re-layouts  11.7 us

profile of v1, /device:TPU:1, one launch (start us, length us, event | category | flops | bytes accessed | tf_op | source)
XLA Modules:
  0.0 117.4 jit_solution(8398853766862415758)
XLA Ops:
  0.6 0.0 copy-start.6
  0.6 1.0 convert_reduce_fusion
  1.6 0.7 iota_add_fusion
  2.3 0.1 select_reduce_fusion.1
  2.4 0.1 copy.29
  2.5 0.8 fusion.4
  3.3 0.1 copy.27
  3.4 0.1 copy.30
  3.5 0.7 reshape.96.new_keys
  4.2 0.7 reshape.97.new_values
  4.9 0.8 select_reduce_fusion
  5.7 0.1 copy.32
  5.8 0.1 multiply_reduce_fusion
  5.9 0.1 copy.28
  6.0 0.1 copy.31
  6.1 0.7 reshape.98.residual
  6.9 0.2 multiply_convert_fusion
  7.1 0.1 convert_element_type.41.scatter
  7.3 0.9 reshape.95.queries
  8.2 0.3 broadcast_multiply_fusion
  8.5 0.3 mul.76
  8.8 0.1 copy.35.gather
  8.9 0.0 copy-done.6
  8.9 2.5 %copy.33 = bf16[1,4096,192]{2,1,0:T(8,128)(2,1)} copy(bf16[1,4096,192]{1,2,0:T(8,128)(2,1)S(1)} %copy-done.6) | data formatting | bytes 3145728 | tf_op args[12]
  11.4 0.0 copy-start
  11.4 0.0 copy-start.2
  11.4 0.0 copy-start.4
  11.4 0.0 copy-start.5
  11.4 4.0 %copy.34 = bf16[1,4096,192]{2,1,0:T(8,128)(2,1)} copy(bf16[1,4096,192]{1,2,0:T(8,128)(2,1)} %param.28) | data formatting | bytes 3145728 | tf_op args[13]
  15.4 0.0 copy-done
  15.4 0.0 copy-done.2
  15.4 0.0 copy-done.4
  15.4 0.0 copy-done.5
  15.5 0.0 copy-start.3
  15.5 1.0 copy-done.3
  16.5 96.1 %shard_map.166 = (bf16[128,16,256]{2,1,0:T(8,128)(2,1)S(1)}, bf16[128,16,256]{2,1,0:T(8,128)(2,1)S(1)}, bf16[16,512]{1,0:T(8,128)(2,1)S(1)}) custom-call(s32[128]{0:T(128)S(1)} %broadcast_add_fusion.inverse, s32[4]{0:T(128)S(1)} %copy-done.5, bf16[16,4096]{1,0:T(8,128)(2,1)S(1)} %reshape.95.queries, bf16[16,256]{1,0:T(8,128)(2,1)S(1)} %reshape.96.new_keys, ...), custom_call_target="tpu_custom_call" | custom-call | tf_op jit(solution)/shard_map/pallas_call | solution.py:463
  112.6 0.0 copy-start.1
  112.6 1.0 copy-done.1
  113.5 0.6 reshape.99
  114.2 2.3 %copy.38 = bf16[128,16,256]{2,1,0:T(8,128)(2,1)} copy(bf16[128,16,256]{2,1,0:T(8,128)(2,1)} %copy-done.1) | data formatting | bytes 2097152
  116.4 1.0 copy.39
  (6 shorter events, 0.1 us)
Async XLA Ops:
  0.6 8.3 %copy-start.6 = (bf16[1,4096,192]{1,2,0:T(8,128)(2,1)S(1)}, bf16[1,4096,192]{1,2,0:T(8,128)(2,1)}, u32[]{:S(2)}) copy-start(bf16[1,4096,192]{1,2,0:T(8,128)(2,1)} %param.27) | copy-start | bytes 4718596
  11.4 4.0 %copy-start = (bf16[1,192,4096]{2,1,0:T(8,128)(2,1)S(1)}, bf16[1,192,4096]{2,1,0:T(8,128)(2,1)}, u32[]{:S(2)}) copy-start(bf16[1,192,4096]{2,1,0:T(8,128)(2,1)} %param.29) | copy-start | bytes 4718596
  11.4 4.0 %copy-start.2 = (bf16[64,16,256]{2,1,0:T(8,128)(2,1)S(1)}, bf16[64,16,256]{2,1,0:T(8,128)(2,1)}, u32[]{:S(2)}) copy-start(bf16[64,16,256]{2,1,0:T(8,128)(2,1)} %keys.1) | copy-start | bytes 1572868
  11.4 4.0 %copy-start.4 = (f32[512]{0:T(512)S(1)}, f32[512]{0:T(512)}, u32[]{:S(2)}) copy-start(f32[512]{0:T(512)} %param.24) | copy-start | bytes 6148
  11.4 4.0 %copy-start.5 = (s32[4]{0:T(128)S(1)}, s32[4]{0:T(128)}, u32[]{:S(2)}) copy-start(s32[4]{0:T(128)} %lengths.1) | copy-start | bytes 52
  15.5 1.0 copy-start.3
  112.6 1.0 copy-start.1

commit v2 on v1

v2 whole, which is shorter than its diff:
```python
import math

import jax
import jax.numpy as jnp
from jax import lax
from jax.experimental import pallas as pl
from jax.experimental.pallas import tpu as pltpu
from jax.sharding import PartitionSpec as P

MESH = pl.DeviceIdType.MESH
F32 = jnp.float32
BF16 = jnp.bfloat16

DP = 32
TP = 8
HEAD = 128
TOKENS = 16
SLOTS = 6
PAD_SLOTS = 8
ROWS = DP * SLOTS
SUBS = 4
SUB_ROWS = ROWS // SUBS
MESSAGES = 7 * SUBS // 2
PART = 512
WIDE = 256
BLOCK = 16
EPSILON = 1e-06
LOW = -1e30
EARLY = 10


def iota(shape, dim):
    return lax.broadcasted_iota(jnp.int32, shape, dim)


def onehot(mask):
    return jnp.where(mask, 1.0, 0.0).astype(BF16)


def dot(a, b):
    return jnp.dot(a, b, preferred_element_type=F32)


def dot_last(a, b):
    return lax.dot_general(a, b, (((1,), (1,)), ((), ())), preferred_element_type=F32)


def split_three(value):
    top = value.astype(BF16).astype(F32)
    rest = value - top
    middle = rest.astype(BF16).astype(F32)
    return top, middle, rest - middle


def layer_kernel(
    lengths, page_dest_in, queries_in, new_keys_in, new_values_in, residual_in, gain_in, ids_in,
    probs_in, keys, values, out_weight, w_gate, w_up, w_down,
    moved_keys, moved_values, layer_out,
    page_dest, queries, new_keys, new_values, residual, gain, ids, probs,
    qrows, idrows, new_rows, inverse_row, inverse, pick_in, pick_out,
    kbuf, vbuf, ksend, vsend, wo, wg, wu, wd,
    part_send, part_recv, coeff, attended, state,
    disp_send, disp_recv, xbuf, sqbuf, gate_acc, up_acc, ybuf,
    lsend, rsend, lrecv, rrecv, ret_send, ret_recv,
    local_sem, page_send_sem, page_recv_sem, part_ssem, part_rsem, att_ssem, att_rsem,
    disp_ssem, disp_rsem, sq_ssem, sq_rsem, ring_ssem, ring_rsem, red_ssem, red_rsem,
    ret_ssem, ret_rsem,
):
    me = lax.axis_index("dp")
    t = lax.axis_index("tp")

    def local(src, dst, i):
        return pltpu.make_async_copy(src, dst, local_sem.at[i])

    small = [
        local(src, dst, 8 + i)
        for i, (src, dst) in enumerate((
            (page_dest_in, page_dest), (queries_in, queries), (new_keys_in, new_keys),
            (new_values_in, new_values), (residual_in, residual), (gain_in, gain),
            (ids_in, ids), (probs_in, probs),
        ))
    ]
    loads = [
        local(keys, kbuf.at[pl.ds(0, 64)], 0),
        local(values, vbuf.at[pl.ds(0, 64)], 1),
        local(out_weight, wo, 2),
        local(w_gate, wg, 3),
        local(w_up, wu, 4),
        local(w_down, wd, 5),
    ]
    for load in small + loads:
        load.start()

    barrier = pltpu.get_barrier_semaphore()

    @pl.loop(1, DP)
    def _(d):
        pl.semaphore_signal(
            barrier, inc=1, device_id=(lax.rem(me + d, DP), t), device_id_type=MESH
        )

    for d in range(1, TP):
        pl.semaphore_signal(
            barrier, inc=1, device_id=(me, lax.rem(t + d, TP)), device_id_type=MESH
        )

    kbuf[64] = jnp.zeros((16, WIDE), BF16)
    vbuf[64] = jnp.zeros((16, WIDE), BF16)
    for load in small:
        load.wait()

    def rows_together(ref, scratch):
        for r in range(4):
            scratch[4 * r : 4 * r + 4, : ref.shape[2]] = ref[r].astype(F32)
        return scratch[:, : ref.shape[2]]

    rows_together(new_keys, new_rows.at[0])
    rows_together(new_values, new_rows.at[1])
    residual_rows = rows_together(residual, idrows)
    rows_together(queries, qrows)

    loads[0].wait()
    loads[1].wait()

    row = iota((256, 256), 0)
    col = iota((256, 256), 1)
    perm = onehot(col == ((row >> 2) & 15) * 16 + (row >> 6) * 4 + (row & 3))
    perm_back = onehot(col == ((row >> 2) & 3) * 64 + (row >> 4) * 4 + (row & 3))
    scale = 1.0 / math.sqrt(HEAD)
    lane = iota((64, 256), 1)
    position = (lane >> 4) * 128 + t * 16 + (lane & 15)
    frow = iota((256, TOKENS), 0)
    fcol = iota((256, TOKENS), 1)
    fvisible = ((fcol >> 2) == (frow >> 6)) & ((fcol & 3) <= (frow & 3)) & (t == 0)
    stat_lane = iota((256, HEAD), 1)

    def part_copy(d):
        dest = lax.rem(t + d, TP)
        return pltpu.make_async_remote_copy(
            src_ref=part_send.at[dest],
            dst_ref=part_recv.at[t],
            send_sem=part_ssem.at[d],
            recv_sem=part_rsem.at[t],
            device_id=(me, dest),
            device_id_type=MESH,
        )

    def attend(k):
        cols = pl.ds(pl.multiple_of(k * HEAD, HEAD), HEAD)
        q_rows = jnp.concatenate(
            [
                qrows[:, pl.ds(pl.multiple_of((k * 16 + g) * HEAD, HEAD), HEAD)]
                for g in range(16)
            ],
            axis=0,
        )
        q_rows = dot(perm, q_rows.astype(BF16)).astype(BF16)
        fresh_k = new_rows[0, :, cols].astype(BF16)
        fresh_v = new_rows[1, :, cols].astype(BF16)
        scores = []
        for r in range(4):
            k_r = kbuf[16 * r : 16 * r + 16, :, cols].reshape(256, HEAD)
            score = dot_last(q_rows[64 * r : 64 * r + 64], k_r) * scale
            scores.append(jnp.where(position < lengths[r], score, LOW))
        scores = jnp.concatenate(scores, axis=0)
        fscores = jnp.where(fvisible, dot_last(q_rows, fresh_k) * scale, LOW)
        top = jnp.maximum(
            jnp.max(scores, axis=1, keepdims=True), jnp.max(fscores, axis=1, keepdims=True)
        )
        weights = jnp.exp(scores - top)
        fweights = jnp.exp(fscores - top)
        total = jnp.sum(weights, axis=1, keepdims=True) + jnp.sum(fweights, axis=1, keepdims=True)
        weights = weights.astype(BF16)
        accs = [
            dot(
                weights[64 * r : 64 * r + 64],
                vbuf[16 * r : 16 * r + 16, :, cols].reshape(256, HEAD),
            )
            for r in range(4)
        ]
        acc = jnp.concatenate(accs, axis=0) + dot(fweights.astype(BF16), fresh_v)
        acc = dot(perm_back, acc.astype(BF16)).astype(BF16)
        stats = jnp.zeros((256, HEAD), F32)
        for i, piece in enumerate(split_three(top) + split_three(total)):
            stats = jnp.where(stat_lane == i, piece, stats)
        stats = jnp.transpose(stats)[0:16].astype(BF16)
        stats = dot(stats, perm).astype(BF16)
        for q in range(4):
            part_send[k * 4 + q, 0:64] = acc[64 * q : 64 * q + 64]
            part_send[k * 4 + q, 64:80] = stats[:, 128 * (q >> 1) : 128 * (q >> 1) + 128]

    far = 1 - (t >> 2)
    attend(far)
    pl.semaphore_wait(barrier, DP - 1 + TP - 1)
    mine_at = t & 3
    for q in range(4):
        part_copy(lax.rem(far * 4 + q + TP - t, TP)).start()
    attend(1 - far)
    for q in range(1, 4):
        part_copy(lax.rem((1 - far) * 4 + ((mine_at + q) & 3) + TP - t, TP)).start()

    def wait_recv(ref, sem):
        pltpu.make_async_copy(ref, ref, sem).wait()

    pending = []

    def finish():
        for wait in pending:
            wait()
        pending.clear()

    def finish_parts():
        for d in range(1, TP):
            part_copy(d).wait_send()

    pending.append(finish_parts)
    part_recv[t] = part_send[t]

    dest = jnp.broadcast_to(page_dest[...], (64, 64))
    page_row = iota((64, 64), 0)
    page_col = iota((64, 64), 1)
    dest_of = jnp.sum(jnp.where(page_row == page_col, dest, 0), axis=1, keepdims=True)
    earlier = (dest == dest_of) & (page_col < page_row)
    within = jnp.sum(jnp.where(earlier, 1, 0), axis=1, keepdims=True)
    hit = dest_of * 4 + within == iota((64, 128), 1)
    number = iota((64, 128), 0) - 64
    inverse_row[...] = 64 + jnp.sum(jnp.where(hit, number, 0), axis=0, keepdims=True)
    to_scalars = local(inverse_row, inverse, 16)
    to_scalars.start()

    to_scalars.wait()

    @pl.loop(0, 128)
    def _(slot):
        page = jnp.clip(inverse[0, slot], 0, 64)
        ksend[slot] = kbuf[page]
        vsend[slot] = vbuf[page]

    def page_copy(which, d):
        dest = lax.rem(me + d, DP)
        src, dst = ((ksend, moved_keys), (vsend, moved_values))[which]
        return pltpu.make_async_remote_copy(
            src_ref=src.at[pl.ds(dest * 4, 4)],
            dst_ref=dst.at[pl.ds(me * 4, 4)],
            send_sem=page_send_sem.at[which],
            recv_sem=page_recv_sem.at[which],
            device_id=(dest, t),
            device_id_type=MESH,
        )

    def send_pages(first, last):
        @pl.loop(first, last)
        def _(d):
            page_copy(0, d).start()
            page_copy(1, d).start()

    send_pages(1, EARLY)

    own_k = local(ksend.at[pl.ds(me * 4, 4)], moved_keys.at[pl.ds(me * 4, 4)], 6)
    own_v = local(vsend.at[pl.ds(me * 4, 4)], moved_values.at[pl.ds(me * 4, 4)], 7)
    own_k.start()
    own_v.start()

    def finish_pages():
        own_k.wait()
        own_v.wait()

        others = pl.ds(0, 4 * (DP - 1))
        for which, ref in enumerate((moved_keys, moved_values)):
            wait_recv(ref.at[others], page_recv_sem.at[which])
            wait_recv(ref.at[others], page_send_sem.at[which])


    for d in range(1, TP):
        src = lax.rem(t + d, TP)
        wait_recv(part_recv.at[src], part_rsem.at[src])
    tops, sums = [], []
    for s in range(TP):
        stat = part_recv[s, 64:80].astype(F32)
        tops.append(stat[0:1] + stat[1:2] + stat[2:3])
        sums.append(stat[3:4] + stat[4:5] + stat[5:6])
    tops = jnp.concatenate(tops, axis=0)
    sums = jnp.concatenate(sums, axis=0)
    scales = jnp.exp(tops - jnp.max(tops, axis=0, keepdims=True))
    scales = scales / jnp.sum(scales * sums, axis=0, keepdims=True)
    scales = jnp.concatenate([scales, jnp.zeros((120, HEAD), F32)], axis=0)
    coeff[...] = jnp.transpose(scales)
    mine = coeff[pl.ds(pl.multiple_of((t & 1) * 64, 64), 64), :]
    merged = jnp.zeros((64, HEAD), F32)
    for s in range(TP):
        merged = merged + mine[:, s : s + 1] * part_recv[s, 0:64].astype(F32)
    merged = merged.astype(BF16)
    for h in range(4):
        attended[t, :, h * HEAD : (h + 1) * HEAD] = merged[h * 16 : h * 16 + 16]

    def att_copy(d):
        return pltpu.make_async_remote_copy(
            src_ref=attended.at[t],
            dst_ref=attended.at[t],
            send_sem=att_ssem.at[d],
            recv_sem=att_rsem.at[t],
            device_id=(me, lax.rem(t + d, TP)),
            device_id_type=MESH,
        )

    def send_att(d):
        att_copy(d).start()
        pending.append(lambda: att_copy(d).wait_send())

    for d in range(1, TP):
        send_att(d)

    named = rows_together(ids, idrows)
    prob = rows_together(probs, idrows)
    expert = iota((TOKENS, DP), 1).astype(F32)
    member = jnp.zeros((TOKENS, DP), F32)
    weight = jnp.zeros((TOKENS, DP), F32)
    for j in range(8):
        same = named[:, j : j + 1] == expert
        member = member + jnp.where(same, 1.0, 0.0)
        weight = weight + jnp.where(same, prob[:, j : j + 1], 0.0)
    member = member.astype(BF16)
    below = onehot(iota((TOKENS, TOKENS), 1) < iota((TOKENS, TOKENS), 0))
    rank = dot(below, member).astype(BF16)
    lane_expert = onehot((iota((DP, DP * BLOCK), 1) >> 4) == iota((DP, DP * BLOCK), 0))
    lane = iota((TOKENS, DP * BLOCK), 1)
    chosen = jnp.where(
        dot(rank, lane_expert) == (lane & 7).astype(F32), dot(member, lane_expert), 0.0
    )
    first = jnp.where((lane & 8) == 0, chosen, 0.0)
    scatter_back = jnp.concatenate([first, chosen - first], axis=0)
    scatter = jnp.transpose(scatter_back).astype(BF16)
    weight_top = weight.astype(BF16)
    weight_rest = (weight - weight_top.astype(F32)).astype(BF16)
    gather_top, gather_rest = [
        jnp.concatenate([part, part], axis=0) for part in (
            dot(weight_top, lane_expert), dot(weight_rest, lane_expert))
    ]
    gather_top = (gather_top * scatter_back).astype(BF16)
    gather_rest = (gather_rest * scatter_back).astype(BF16)

    prow = iota((ROWS, DP * BLOCK), 0)
    pcol = iota((ROWS, DP * BLOCK), 1)
    place = (prow & 31) * BLOCK + (prow >> 5)
    rrow = iota((DP * BLOCK, ROWS), 0)
    rcol = iota((DP * BLOCK, ROWS), 1)
    rplace = (rrow & 7) * DP + (rrow >> 4)
    for h in range(2):
        pick_in[h] = onehot(pcol == place + h * PAD_SLOTS)
        pick_out[h] = onehot((rcol == rplace) & (((rrow >> 3) & 1) == h))

    loads[2].wait()

    def project(src):
        return dot(attended[src], wo[pl.ds(pl.multiple_of(src * PART, PART), PART), :])

    projected = project(t)
    for d in (1, 7, 2, 6, 3, 5, 4):
        src = lax.rem(t + d, TP)
        wait_recv(attended.at[src], att_rsem.at[src])
        projected = projected + project(src)
    layer_state = (residual_rows + projected).astype(BF16)
    state[...] = layer_state

    stacked = jnp.concatenate([layer_state[:, :WIDE], layer_state[:, WIDE:]], axis=0)
    disp_send[...] = dot(scatter, stacked).astype(BF16)

    def block_of(ref, rank):
        return ref.at[pl.ds(pl.multiple_of(rank * BLOCK, BLOCK), BLOCK)]

    def all_copy(send, recv, ssem, rsem, d):
        dest = lax.rem(me + d, DP)
        return pltpu.make_async_remote_copy(
            src_ref=block_of(send, dest),
            dst_ref=block_of(recv, me),
            send_sem=ssem.at[0],
            recv_sem=rsem.at[0],
            device_id=(dest, t),
            device_id_type=MESH,
        )

    def exchange(send, recv, ssem, rsem):
        @pl.loop(1, DP)
        def _(d):
            all_copy(send, recv, ssem, rsem, d).start()

        block = pl.ds(pl.multiple_of(me * BLOCK, BLOCK), BLOCK)
        recv[block, :] = send[block, :]
        finish()
        others = pl.ds(0, BLOCK * (DP - 1))
        wait_recv(recv.at[others], rsem.at[0])
        pending.append(lambda: wait_recv(send.at[others], ssem.at[0]))

    exchange(disp_send, disp_recv, disp_ssem, disp_rsem)
    send_pages(EARLY, DP)
    pending.append(finish_pages)

    arrived = disp_recv[...]
    pieces = [dot(pick_in[h], arrived) for h in range(2)]
    for h in range(2):
        features = slice(h * WIDE, (h + 1) * WIDE)
        xbuf[t, :, features] = (pieces[h] * gain[:, features]).astype(BF16)
    toward = (lax.rem(t + 1, TP), lax.rem(t + TP - 1, TP))

    def rows_of(way, i):
        sub = i % SUBS
        return pl.ds((sub if way == 0 else SUBS - 1 - sub) * SUB_ROWS, SUB_ROWS)

    def ring_piece(way, i, step):
        chunk = lax.rem(t + (TP - step if way == 0 else step), TP)
        return xbuf.at[chunk, rows_of(way, i)]

    def ring_copy(way, i):
        piece = ring_piece(way, i, i // SUBS)
        return pltpu.make_async_remote_copy(
            src_ref=piece,
            dst_ref=piece,
            send_sem=ring_ssem.at[way, i],
            recv_sem=ring_rsem.at[way, i],
            device_id=(me, toward[way]),
            device_id_type=MESH,
        )

    def ring_wait(way, i):
        wait_recv(ring_piece(way, i, i // SUBS + 1), ring_rsem.at[way, i])

    def expert_in(chunk, first=False):
        x = xbuf[chunk]
        features = pl.ds(pl.multiple_of(chunk * PART, PART), PART)
        gate_part = dot_last(x, wg[:, features])
        up_part = dot_last(x, wu[:, features])
        if first:
            gate_acc[...] = gate_part
            up_acc[...] = up_part
        else:
            gate_acc[...] += gate_part
            up_acc[...] += up_part

    def send_ring(way, i):
        ring_copy(way, i).start()
        pending.append(lambda: ring_copy(way, i).wait_send())

    for i in range(SUBS):
        for way in range(2):
            send_ring(way, i)

    square = jnp.sum(pieces[0] * pieces[0], axis=1, keepdims=True)
    square = square + jnp.sum(pieces[1] * pieces[1], axis=1, keepdims=True)
    square = jnp.concatenate([square, jnp.zeros((256 - ROWS, 1), F32)], axis=0)
    sqbuf[t] = jnp.transpose(jnp.broadcast_to(square, (256, HEAD)))[0:1]

    def sq_copy(d):
        return pltpu.make_async_remote_copy(
            src_ref=sqbuf.at[t],
            dst_ref=sqbuf.at[t],
            send_sem=sq_ssem.at[d],
            recv_sem=sq_rsem.at[t],
            device_id=(me, lax.rem(t + d, TP)),
            device_id_type=MESH,
        )

    def send_sq(d):
        sq_copy(d).start()
        pending.append(lambda: sq_copy(d).wait_send())

    for d in range(1, TP):
        send_sq(d)

    loads[3].wait()
    loads[4].wait()
    expert_in(t, first=True)
    for i in range(MESSAGES):
        for way in range(2):
            ring_wait(way, i)
            if i + SUBS < MESSAGES:
                send_ring(way, i + SUBS)
        if i % SUBS == SUBS - 1:
            expert_in(lax.rem(t + TP - (i // SUBS + 1), TP))
            expert_in(lax.rem(t + i // SUBS + 1, TP))
    expert_in(lax.rem(t + 4, TP))

    for d in range(1, TP):
        src = lax.rem(t + d, TP)
        wait_recv(sqbuf.at[src], sq_rsem.at[src])
    total = sqbuf[0]
    for s in range(1, TP):
        total = total + sqbuf[s]
    inv_norm = lax.rsqrt(total * (1.0 / (TP * PART)) + EPSILON)
    inv_norm = jnp.transpose(jnp.broadcast_to(inv_norm, (HEAD, 256)))[0:ROWS, 0:1]
    gate_part = gate_acc[...] * inv_norm
    up_part = up_acc[...] * inv_norm
    hidden = (gate_part / (1.0 + jnp.exp(-gate_part)) * up_part).astype(BF16)

    loads[5].wait()
    sends = (rsend, lsend)
    recvs = (rrecv, lrecv)

    def expert_out(chunk):
        ybuf[chunk] = dot(hidden, wd[:, pl.ds(pl.multiple_of(chunk * PART, PART), PART)])

    def red_copy(way, j):
        return pltpu.make_async_remote_copy(
            src_ref=sends[way].at[j],
            dst_ref=recvs[way].at[j],
            send_sem=red_ssem.at[way, j],
            recv_sem=red_rsem.at[way, j],
            device_id=(me, toward[way]),
            device_id_type=MESH,
        )

    def send_red(way, j):
        red_copy(way, j).start()
        pending.append(lambda: red_copy(way, j).wait_send())

    for j in range(MESSAGES):
        step = (j + SUBS // 2) // SUBS
        sub_at = (j + SUBS // 2) % SUBS
        for way in range(2):
            distance = 4 - step
            chunk = lax.rem(t + (distance if way == 0 else TP - distance), TP)
            if sub_at == 0 or (j == 0 and way == 0):
                expert_out(chunk)
            sub = sub_at if way == 0 else SUBS - 1 - sub_at
            value = ybuf[chunk, sub * SUB_ROWS : (sub + 1) * SUB_ROWS]
            if j >= SUBS:
                wait_recv(recvs[way].at[j - SUBS], red_rsem.at[way, j - SUBS])
                value = value + recvs[way][j - SUBS].astype(F32)
            sends[way][j] = value.astype(BF16)
            send_red(way, j)
    expert_out(t)
    for j in range(MESSAGES - SUBS, MESSAGES):
        for way in range(2):
            wait_recv(recvs[way].at[j], red_rsem.at[way, j])
    results = []
    for sub in range(SUBS):
        value = ybuf[t, sub * SUB_ROWS : (sub + 1) * SUB_ROWS]
        value = value + recvs[0][MESSAGES - SUBS + sub].astype(F32)
        value = value + recvs[1][MESSAGES - 1 - sub].astype(F32)
        results.append(value.astype(BF16))
    result = jnp.concatenate(results, axis=0)

    back = dot(pick_out[0], result[:, :WIDE]) + dot(pick_out[1], result[:, WIDE:])
    ret_send[...] = back.astype(BF16)
    exchange(ret_send, ret_recv, ret_ssem, ret_rsem)

    returned = ret_recv[...]
    mixture = dot(gather_top, returned) + dot(gather_rest, returned)
    for h in range(2):
        features = slice(h * WIDE, (h + 1) * WIDE)
        total = state[:, features].astype(F32) + mixture[h * TOKENS : (h + 1) * TOKENS]
        for r in range(4):
            layer_out[r, :, features] = total[4 * r : 4 * r + 4].astype(BF16)

    finish()


def layer(*operands):
    smem = pl.BlockSpec(memory_space=pltpu.SMEM)
    vmem = pl.BlockSpec(memory_space=pltpu.VMEM)
    hbm = pl.BlockSpec(memory_space=pltpu.HBM)
    anywhere = pl.BlockSpec(memory_space=pl.ANY)
    dma = pltpu.SemaphoreType.DMA
    return pl.pallas_call(
        layer_kernel,
        out_shape=(
            jax.ShapeDtypeStruct((128, 16, WIDE), BF16),
            jax.ShapeDtypeStruct((128, 16, WIDE), BF16),
            jax.ShapeDtypeStruct((4, 4, PART), BF16),
        ),
        in_specs=[smem] + [hbm] * 14,
        out_specs=(anywhere, anywhere, vmem),
        scratch_shapes=[
            pltpu.VMEM((1, 64), jnp.int32),
            pltpu.VMEM((4, 4, 4096), BF16),
            pltpu.VMEM((4, 4, WIDE), BF16),
            pltpu.VMEM((4, 4, WIDE), BF16),
            pltpu.VMEM((4, 4, PART), BF16),
            pltpu.VMEM((1, PART), F32),
            pltpu.VMEM((4, 4, 8), jnp.int32),
            pltpu.VMEM((4, 4, 8), F32),
            pltpu.VMEM((TOKENS, 4096), F32),
            pltpu.VMEM((TOKENS, PART), F32),
            pltpu.VMEM((2, TOKENS, WIDE), F32),
            pltpu.VMEM((1, 128), jnp.int32),
            pltpu.SMEM((1, 128), jnp.int32),
            pltpu.VMEM((2, ROWS, DP * BLOCK), BF16),
            pltpu.VMEM((2, DP * BLOCK, ROWS), BF16),
            pltpu.VMEM((65, 16, WIDE), BF16),
            pltpu.VMEM((65, 16, WIDE), BF16),
            pltpu.VMEM((128, 16, WIDE), BF16),
            pltpu.VMEM((128, 16, WIDE), BF16),
            pltpu.VMEM((4096, PART), BF16),
            pltpu.VMEM((192, 4096), BF16),
            pltpu.VMEM((192, 4096), BF16),
            pltpu.VMEM((192, 4096), BF16),
            pltpu.VMEM((TP, 80, HEAD), BF16),
            pltpu.VMEM((TP, 80, HEAD), BF16),
            pltpu.VMEM((HEAD, HEAD), F32),
            pltpu.VMEM((TP, TOKENS, PART), BF16),
            pltpu.VMEM((TOKENS, PART), BF16),
            pltpu.VMEM((DP * BLOCK, WIDE), BF16),
            pltpu.VMEM((DP * BLOCK, WIDE), BF16),
            pltpu.VMEM((TP, ROWS, PART), BF16),
            pltpu.VMEM((TP, 1, 256), F32),
            pltpu.VMEM((ROWS, 192), F32),
            pltpu.VMEM((ROWS, 192), F32),
            pltpu.VMEM((TP, ROWS, PART), F32),
            pltpu.VMEM((MESSAGES, SUB_ROWS, PART), BF16),
            pltpu.VMEM((MESSAGES, SUB_ROWS, PART), BF16),
            pltpu.VMEM((MESSAGES, SUB_ROWS, PART), BF16),
            pltpu.VMEM((MESSAGES, SUB_ROWS, PART), BF16),
            pltpu.VMEM((DP * BLOCK, WIDE), BF16),
            pltpu.VMEM((DP * BLOCK, WIDE), BF16),
            dma((17,)),
            dma((2,)), dma((2,)),
            dma((TP,)), dma((TP,)), dma((TP,)), dma((TP,)),
            dma((1,)), dma((1,)),
            dma((TP,)), dma((TP,)),
            dma((2, MESSAGES)), dma((2, MESSAGES)), dma((2, MESSAGES)), dma((2, MESSAGES)),
            dma((1,)), dma((1,)),
        ],
        compiler_params=pltpu.CompilerParams(
            collective_id=0, has_side_effects=True, vmem_limit_bytes=60 * 1024 * 1024
        ),
    )(*operands)


def place_kernel(keys, values, rows, keys_out, values_out, rows_out, kbuf, vbuf, rbuf, sems):
    moves = [(rows, rbuf, rows_out)]
    for i in range(4):
        for src, buf, dst in ((keys, kbuf, keys_out), (values, vbuf, values_out)):
            part = pl.ds(i * 32, 32)
            moves.append((src.at[part], buf.at[part], dst.at[part]))
    loads = [
        pltpu.make_async_copy(src, buf, sems.at[0, i]) for i, (src, buf, _) in enumerate(moves)
    ]
    stores = [
        pltpu.make_async_copy(buf, dst, sems.at[1, i]) for i, (_, buf, dst) in enumerate(moves)
    ]
    for load in loads:
        load.start()
    for load, store in zip(loads, stores):
        load.wait()
        store.start()
    for store in stores:
        store.wait()


def place(*arrays):
    hbm = pl.BlockSpec(memory_space=pltpu.HBM)
    return pl.pallas_call(
        place_kernel,
        out_shape=tuple(jax.ShapeDtypeStruct(a.shape, a.dtype) for a in arrays),
        in_specs=[pl.BlockSpec(memory_space=pl.ANY)] * 3,
        out_specs=(hbm,) * 3,
        scratch_shapes=[pltpu.VMEM(a.shape, a.dtype) for a in arrays]
        + [pltpu.SemaphoreType.DMA((2, 9))],
        compiler_params=pltpu.CompilerParams(vmem_limit_bytes=60 * 1024 * 1024),
    )(*arrays)


def shards(
    cache_keys, cache_values, page_dest, lengths, queries, new_keys, new_values, residual,
    out_weight, norm_gain, expert_ids, gate_probs, w_gate, w_up, w_down,
):
    return place(*layer(
        lengths,
        page_dest.reshape(1, -1),
        queries,
        new_keys,
        new_values,
        residual,
        norm_gain[None, :],
        expert_ids,
        gate_probs,
        cache_keys,
        cache_values,
        out_weight,
        w_gate[0].T,
        w_up[0].T,
        w_down[0],
    ))


def solution(mesh):
    in_specs = (
        P("dp", "tp", None),
        P("dp", "tp", None),
        P("dp", None),
        P("dp"),
        P("dp", None, None),
        P("dp", None, None),
        P("dp", None, None),
        P("dp", None, "tp"),
        P(None, "tp"),
        P("tp"),
        P("dp", None, None),
        P("dp", None, None),
        P("dp", None, "tp"),
        P("dp", None, "tp"),
        P("dp", "tp", None),
    )
    out_specs = (P("dp", "tp", None), P("dp", "tp", None), P("dp", None, "tp"))
    return jax.shard_map(shards, mesh=mesh, in_specs=in_specs, out_specs=out_specs, check_vma=False)
```

time: 118 us -> 77.8 us (0.66)
  Pallas kernels: 96.1 us -> 77 us
  local copies, waits for them, and re-layouts: 16.5 us -> 0 us
  other arithmetic: 4.08 us -> 0 us
    pallas_call x1, Pallas kernels: 96.1 us -> 74.5 us  [layer(): pl.pallas_call(layer_kernel, out_shape=(jax.ShapeDtypeStruct((128, 16, WI...]
    unnamed x18 -> x0, local copies, waits for them, and re-layouts: 11.7 us -> none
    reshape x5 -> x0, local copies, waits for them, and re-layouts: 3.7 us -> none  [the longest x1 0.94 us: shards(): queries.reshape(TOKENS, -1)]
    pallas_call x0 -> x1, Pallas kernels: none -> 2.43 us  [place(): pl.pallas_call(place_kernel, out_shape=tuple((jax.ShapeDtypeStruct(a.shap...]
    reduce_sum x4 -> x0, other arithmetic: 2 us -> none  [the longest x1 0.97 us: shards(): within = jnp.sum(earlier.astype(jnp.int32), axis=1)]
where the time goes in v2:
time: 77.8 us; the launch traced here: 77.6 us
  Pallas kernels  77 us (99%)
    pallas_call x1, Pallas kernels, layer(): pl.pallas_call(layer_kernel, out_shape=(jax.ShapeDtypeStruct((128, 16, WI...  74.5 us
    pallas_call x1, Pallas kernels, place(): pl.pallas_call(place_kernel, out_shape=tuple((jax.ShapeDtypeStruct(a.shap...  2.43 us

profile of v2, /device:TPU:1, one launch (start us, length us, event | category | flops | bytes accessed | tf_op | source)
XLA Modules:
  0.0 77.6 jit_solution(4278282518030298683)
XLA Ops:
  0.6 74.5 %shard_map.166 = (bf16[128,16,256]{2,1,0:T(8,128)(2,1)}, bf16[128,16,256]{2,1,0:T(8,128)(2,1)}, bf16[4,4,512]{2,1,0:T(4,128)(2,1)}) custom-call(s32[4]{0:T(128)} %lengths.1, s32[1,64]{1,0:T(1,128)} %bitcast.13, bf16[4,4,4096]{2,1,0:T(4,128)(2,1)} %queries_in.1, bf16[4,4,256]{2,1,0:T(4,128)(2,1)} %new_keys_in.1, bf16[4,4,256]{2,1,0:T(4,128)(2,1)} %new_values_in.1, ...), custom_call_target="tpu_custom_call" | custom-call | tf_op jit(solution)/shard_map/pallas_call | solution.py:563
  75.2 2.4 %shard_map.167 = (bf16[128,16,256]{2,1,0:T(8,128)(2,1)}, bf16[128,16,256]{2,1,0:T(8,128)(2,1)}, bf16[4,4,512]{2,1,0:T(4,128)(2,1)}) custom-call(bf16[128,16,256]{2,1,0:T(8,128)(2,1)} %get-tuple-element.6.keys, bf16[128,16,256]{2,1,0:T(8,128)(2,1)} %get-tuple-element.7.values, bf16[4,4,512]{2,1,0:T(4,128)(2,1)} %get-tuple-element.8.rows), custom_call_target="tpu_custom_call" | custom-call | tf_op jit(solution)/shard_map/pallas_call | solution.py:651

commit v3 on v2

--- a/solution.py
+++ b/solution.py
@@ -18,15 +18,23 @@
 SLOTS = 6
 PAD_SLOTS = 8
 ROWS = DP * SLOTS
+BLOCK = 16
+GROUP = 8
+GROUP_ROWS = GROUP * BLOCK
+PART = 512
+WIDE = 256
+EPSILON = 1e-06
+LOW = -1e30
+ARRIVAL = (0, 1, 3, 2)
+RETURN_ORDER = (2, 1, 3, 0)
+RING = 3
+FAR = (4,)
+EARLY = 12
+MIDDLE = 6
+PAGES_A_STEP = 2
 SUBS = 4
 SUB_ROWS = ROWS // SUBS
-MESSAGES = 7 * SUBS // 2
-PART = 512
-WIDE = 256
-BLOCK = 16
-EPSILON = 1e-06
-LOW = -1e30
-EARLY = 10
+MESSAGES = RING * SUBS
 
 
 def iota(shape, dim):
@@ -57,7 +65,8 @@
     probs_in, keys, values, out_weight, w_gate, w_up, w_down,
     moved_keys, moved_values, layer_out,
     page_dest, queries, new_keys, new_values, residual, gain, ids, probs,
-    qrows, idrows, new_rows, inverse_row, inverse, pick_in, pick_out,
+    qrows, idrows, new_rows, inverse_row, inverse, pick_in, pick_out, xwide,
+    far_send, far_recv, fdisp_send, fdisp_recv, fret_send, fret_recv, mix_send, mix_recv,
     kbuf, vbuf, ksend, vsend, wo, wg, wu, wd,
     part_send, part_recv, coeff, attended, state,
     disp_send, disp_recv, xbuf, sqbuf, gate_acc, up_acc, ybuf,
@@ -65,6 +74,7 @@
     local_sem, page_send_sem, page_recv_sem, part_ssem, part_rsem, att_ssem, att_rsem,
     disp_ssem, disp_rsem, sq_ssem, sq_rsem, ring_ssem, ring_rsem, red_ssem, red_rsem,
     ret_ssem, ret_rsem,
+    far_ssem, far_rsem, fdisp_ssem, fdisp_rsem, fret_ssem, fret_rsem, mix_ssem, mix_rsem,
 ):
     me = lax.axis_index("dp")
     t = lax.axis_index("tp")
@@ -88,7 +98,7 @@
         local(w_up, wu, 4),
         local(w_down, wd, 5),
     ]
-    for load in small + loads:
+    for load in small + loads[:2]:
         load.start()
 
     barrier = pltpu.get_barrier_semaphore()
@@ -121,6 +131,8 @@
 
     loads[0].wait()
     loads[1].wait()
+    for load in loads[2:]:
+        load.start()
 
     row = iota((256, 256), 0)
     col = iota((256, 256), 1)
@@ -236,8 +248,10 @@
         ksend[slot] = kbuf[page]
         vsend[slot] = vbuf[page]
 
+    begin = 11 * (me & 1) + 5 * ((me >> 1) & 3) + 8 * (me >> 3)
+
     def page_copy(which, d):
-        dest = lax.rem(me + d, DP)
+        dest = lax.rem(me + 1 + lax.rem(d + begin, DP - 1), DP)
         src, dst = ((ksend, moved_keys), (vsend, moved_values))[which]
         return pltpu.make_async_remote_copy(
             src_ref=src.at[pl.ds(dest * 4, 4)],
@@ -248,28 +262,26 @@
             device_id_type=MESH,
         )
 
+    own_k = local(ksend.at[pl.ds(me * 4, 4)], moved_keys.at[pl.ds(me * 4, 4)], 6)
+    own_v = local(vsend.at[pl.ds(me * 4, 4)], moved_values.at[pl.ds(me * 4, 4)], 7)
+    def finish_pages():
+        own_k.wait()
+        own_v.wait()
+
+        others = pl.ds(0, 4 * (DP - 1))
+        for which, ref in enumerate((moved_keys, moved_values)):
+            wait_recv(ref.at[others], page_recv_sem.at[which])
+            wait_recv(ref.at[others], page_send_sem.at[which])
+
     def send_pages(first, last):
         @pl.loop(first, last)
         def _(d):
             page_copy(0, d).start()
             page_copy(1, d).start()
 
-    send_pages(1, EARLY)
-
-    own_k = local(ksend.at[pl.ds(me * 4, 4)], moved_keys.at[pl.ds(me * 4, 4)], 6)
-    own_v = local(vsend.at[pl.ds(me * 4, 4)], moved_values.at[pl.ds(me * 4, 4)], 7)
     own_k.start()
     own_v.start()
-
-    def finish_pages():
-        own_k.wait()
-        own_v.wait()
-
-        others = pl.ds(0, 4 * (DP - 1))
-        for which, ref in enumerate((moved_keys, moved_values)):
-            wait_recv(ref.at[others], page_recv_sem.at[which])
-            wait_recv(ref.at[others], page_send_sem.at[which])
-
+    send_pages(1, 1 + EARLY)
 
     for d in range(1, TP):
         src = lax.rem(t + d, TP)
@@ -307,7 +319,7 @@
         att_copy(d).start()
         pending.append(lambda: att_copy(d).wait_send())
 
-    for d in range(1, TP):
+    for d in (4, 3, 5, 2, 6, 1, 7):
         send_att(d)
 
     named = rows_together(ids, idrows)
@@ -339,15 +351,17 @@
     gather_top = (gather_top * scatter_back).astype(BF16)
     gather_rest = (gather_rest * scatter_back).astype(BF16)
 
-    prow = iota((ROWS, DP * BLOCK), 0)
-    pcol = iota((ROWS, DP * BLOCK), 1)
-    place = (prow & 31) * BLOCK + (prow >> 5)
-    rrow = iota((DP * BLOCK, ROWS), 0)
-    rcol = iota((DP * BLOCK, ROWS), 1)
-    rplace = (rrow & 7) * DP + (rrow >> 4)
+    prow = iota((SUB_ROWS, GROUP_ROWS), 0)
+    pcol = iota((SUB_ROWS, GROUP_ROWS), 1)
+    source = (prow * 683) >> 12
+    place = source * BLOCK + prow - source * SLOTS
+    rrow = iota((GROUP_ROWS, SUB_ROWS), 0)
+    rcol = iota((GROUP_ROWS, SUB_ROWS), 1)
+    rslot = rrow & 7
+    rplace = (rrow >> 4) * SLOTS + rslot
     for h in range(2):
         pick_in[h] = onehot(pcol == place + h * PAD_SLOTS)
-        pick_out[h] = onehot((rcol == rplace) & (((rrow >> 3) & 1) == h))
+        pick_out[h] = onehot((rcol == rplace) & (rslot < SLOTS) & (((rrow >> 3) & 1) == h))
 
     loads[2].wait()
 
@@ -368,47 +382,102 @@
     def block_of(ref, rank):
         return ref.at[pl.ds(pl.multiple_of(rank * BLOCK, BLOCK), BLOCK)]
 
-    def all_copy(send, recv, ssem, rsem, d):
-        dest = lax.rem(me + d, DP)
-        return pltpu.make_async_remote_copy(
-            src_ref=block_of(send, dest),
-            dst_ref=block_of(recv, me),
-            send_sem=ssem.at[0],
-            recv_sem=rsem.at[0],
-            device_id=(dest, t),
-            device_id_type=MESH,
-        )
-
-    def exchange(send, recv, ssem, rsem):
-        @pl.loop(1, DP)
-        def _(d):
-            all_copy(send, recv, ssem, rsem, d).start()
-
+    group = me >> 3
+
+    def group_at(offset):
+        return (group + offset) & 3
+
+    def blocks_of(ref, count):
+        return ref.at[pl.ds(0, count * BLOCK)]
+
+    def send_group(send, recv, ssem, rsem, offset):
+        for i in range(1 if offset == 0 else 0, GROUP):
+            dest = group_at(offset) * GROUP + ((me + i) & 7)
+            pltpu.make_async_remote_copy(
+                src_ref=block_of(send, dest),
+                dst_ref=block_of(recv, me),
+                send_sem=ssem.at[0],
+                recv_sem=rsem,
+                device_id=(dest, t),
+                device_id_type=MESH,
+            ).start()
+
+    def keep_own(send, recv):
         block = pl.ds(pl.multiple_of(me * BLOCK, BLOCK), BLOCK)
         recv[block, :] = send[block, :]
-        finish()
-        others = pl.ds(0, BLOCK * (DP - 1))
-        wait_recv(recv.at[others], rsem.at[0])
-        pending.append(lambda: wait_recv(send.at[others], ssem.at[0]))
-
-    exchange(disp_send, disp_recv, disp_ssem, disp_rsem)
-    send_pages(EARLY, DP)
-    pending.append(finish_pages)
-
-    arrived = disp_recv[...]
-    pieces = [dot(pick_in[h], arrived) for h in range(2)]
-    for h in range(2):
-        features = slice(h * WIDE, (h + 1) * WIDE)
-        xbuf[t, :, features] = (pieces[h] * gain[:, features]).astype(BF16)
+
+    for offset in ARRIVAL:
+        send_group(disp_send, disp_recv, disp_ssem, disp_rsem.at[group], offset)
+    pending.append(lambda: wait_recv(blocks_of(disp_send, DP - 1), disp_ssem.at[0]))
+    keep_own(disp_send, disp_recv)
+
+    def far_copy(send, recv, ssem, rsem, f, dest):
+        return pltpu.make_async_remote_copy(
+            src_ref=send,
+            dst_ref=recv.at[f],
+            send_sem=ssem.at[f],
+            recv_sem=rsem.at[f],
+            device_id=(me, dest),
+            device_id_type=MESH,
+        )
+
+    far_send[...] = (layer_state.astype(F32) * gain[...]).astype(BF16)
+
+    def start_far(f):
+        copy = far_copy(
+            far_send, far_recv, far_ssem, far_rsem, f, lax.rem(t + FAR[f], TP)
+        )
+        copy.start()
+        pending.append(copy.wait_send)
+
+    for f in range(len(FAR)):
+        start_far(f)
+
+    def far_chunk(f):
+        return lax.rem(t + TP - FAR[f], TP)
+
+    chores = []
+
+    def spread(send, recv, ssem, rsem, f):
+        for offset in ARRIVAL:
+            chores.append(
+                lambda offset=offset: send_group(
+                    send.at[f], recv.at[f], ssem.at[pl.ds(f, 1)], rsem.at[f], offset
+                )
+            )
+        chores.append(lambda: keep_own(send.at[f], recv.at[f]))
+
+    def pass_on(f):
+        def scatter_far():
+            wait_recv(far_recv.at[f], far_rsem.at[f])
+            rows = far_recv[f]
+            rows = jnp.concatenate([rows[:, :WIDE], rows[:, WIDE:]], axis=0)
+            fdisp_send[f] = dot(scatter, rows).astype(BF16)
+
+        chores.append(scatter_far)
+        spread(fdisp_send, fdisp_recv, fdisp_ssem, fdisp_rsem, f)
+        later.append(lambda: wait_recv(blocks_of(fdisp_send.at[f], DP - 1), fdisp_ssem.at[f]))
+
+    later = []
+    for f in range(len(FAR)):
+        pass_on(f)
+    page_chores = []
+    for first in range(1 + EARLY, 1 + EARLY + MIDDLE, PAGES_A_STEP):
+        page_chores.append(lambda first=first: send_pages(first, first + PAGES_A_STEP))
+    chores.extend(page_chores)
+
+    def chore():
+        if chores:
+            chores.pop(0)()
+
+    def rows_at(offset):
+        return pl.ds(pl.multiple_of(group_at(offset) * SUB_ROWS, SUB_ROWS), SUB_ROWS)
+
     toward = (lax.rem(t + 1, TP), lax.rem(t + TP - 1, TP))
-
-    def rows_of(way, i):
-        sub = i % SUBS
-        return pl.ds((sub if way == 0 else SUBS - 1 - sub) * SUB_ROWS, SUB_ROWS)
 
     def ring_piece(way, i, step):
         chunk = lax.rem(t + (TP - step if way == 0 else step), TP)
-        return xbuf.at[chunk, rows_of(way, i)]
+        return xbuf.at[chunk, rows_at(ARRIVAL[i % SUBS])]
 
     def ring_copy(way, i):
         piece = ring_piece(way, i, i // SUBS)
@@ -440,12 +509,21 @@
         ring_copy(way, i).start()
         pending.append(lambda: ring_copy(way, i).wait_send())
 
-    for i in range(SUBS):
+    for at, offset in enumerate(ARRIVAL):
+        count = GROUP - 1 if offset == 0 else GROUP
+        wait_recv(blocks_of(disp_recv, count), disp_rsem.at[group_at(offset)])
+        arrived = disp_recv[
+            pl.ds(pl.multiple_of(group_at(offset) * GROUP_ROWS, GROUP_ROWS), GROUP_ROWS), :
+        ]
+        for h in range(2):
+            features = slice(h * WIDE, (h + 1) * WIDE)
+            piece = dot(pick_in[h], arrived)
+            xwide[rows_at(offset), features] = piece
+            xbuf[t, rows_at(offset), features] = (piece * gain[:, features]).astype(BF16)
         for way in range(2):
-            send_ring(way, i)
-
-    square = jnp.sum(pieces[0] * pieces[0], axis=1, keepdims=True)
-    square = square + jnp.sum(pieces[1] * pieces[1], axis=1, keepdims=True)
+            send_ring(way, at)
+
+    square = jnp.sum(xwide[...] * xwide[...], axis=1, keepdims=True)
     square = jnp.concatenate([square, jnp.zeros((256 - ROWS, 1), F32)], axis=0)
     sqbuf[t] = jnp.transpose(jnp.broadcast_to(square, (256, HEAD)))[0:1]
 
@@ -474,10 +552,21 @@
             ring_wait(way, i)
             if i + SUBS < MESSAGES:
                 send_ring(way, i + SUBS)
+        chore()
         if i % SUBS == SUBS - 1:
             expert_in(lax.rem(t + TP - (i // SUBS + 1), TP))
             expert_in(lax.rem(t + i // SUBS + 1, TP))
-    expert_in(lax.rem(t + 4, TP))
+    while len(chores) > len(page_chores):
+        chore()
+    for f in range(len(FAR)):
+        wait_recv(blocks_of(fdisp_recv.at[f], DP - 1), fdisp_rsem.at[f])
+        for g in range(4):
+            arrived = fdisp_recv[f, g * GROUP_ROWS : (g + 1) * GROUP_ROWS]
+            for h in range(2):
+                xbuf[
+                    far_chunk(f), g * SUB_ROWS : (g + 1) * SUB_ROWS, h * WIDE : (h + 1) * WIDE
+                ] = dot(pick_in[h], arrived).astype(BF16)
+        expert_in(far_chunk(f))
 
     for d in range(1, TP):
         src = lax.rem(t + d, TP)
@@ -512,42 +601,92 @@
         red_copy(way, j).start()
         pending.append(lambda: red_copy(way, j).wait_send())
 
+    def give_back(f):
+        def group_back(offset):
+            if offset == ARRIVAL[0]:
+                expert_out(far_chunk(f))
+            value = ybuf[far_chunk(f), rows_at(offset), :].astype(BF16)
+            back = dot(pick_out[0], value[:, :WIDE]) + dot(pick_out[1], value[:, WIDE:])
+            rows = pl.ds(pl.multiple_of(group_at(offset) * GROUP_ROWS, GROUP_ROWS), GROUP_ROWS)
+            fret_send[f, rows, :] = back.astype(BF16)
+            send_group(
+                fret_send.at[f], fret_recv.at[f], fret_ssem.at[pl.ds(f, 1)], fret_rsem.at[f], offset
+            )
+
+        def mix_far():
+            wait_recv(blocks_of(fret_recv.at[f], DP - 1), fret_rsem.at[f])
+            returned = fret_recv[f]
+            mixture = dot(gather_top, returned) + dot(gather_rest, returned)
+            for h in range(2):
+                mix_send[f, :, h * WIDE : (h + 1) * WIDE] = mixture[
+                    h * TOKENS : (h + 1) * TOKENS
+                ].astype(BF16)
+            copy = far_copy(mix_send.at[f], mix_recv, mix_ssem, mix_rsem, f, far_chunk(f))
+            copy.start()
+            pending.append(copy.wait_send)
+
+        for offset in ARRIVAL:
+            urgent.append(lambda offset=offset: group_back(offset))
+        urgent.append(lambda: keep_own(fret_send.at[f], fret_recv.at[f]))
+        mixing.append(mix_far)
+        later.append(lambda: wait_recv(blocks_of(fret_send.at[f], DP - 1), fret_ssem.at[f]))
+
+    urgent, mixing = [], []
+    for f in range(len(FAR)):
+        give_back(f)
+    chores.extend(urgent)
+    chores.append(lambda: send_pages(1 + EARLY + MIDDLE, DP))
+    chores.extend(mixing)
     for j in range(MESSAGES):
-        step = (j + SUBS // 2) // SUBS
-        sub_at = (j + SUBS // 2) % SUBS
+        distance = RING - j // SUBS
+        offset = RETURN_ORDER[j % SUBS]
         for way in range(2):
-            distance = 4 - step
             chunk = lax.rem(t + (distance if way == 0 else TP - distance), TP)
-            if sub_at == 0 or (j == 0 and way == 0):
+            if j % SUBS == 0:
                 expert_out(chunk)
-            sub = sub_at if way == 0 else SUBS - 1 - sub_at
-            value = ybuf[chunk, sub * SUB_ROWS : (sub + 1) * SUB_ROWS]
+            value = ybuf[chunk, rows_at(offset), :]
             if j >= SUBS:
                 wait_recv(recvs[way].at[j - SUBS], red_rsem.at[way, j - SUBS])
                 value = value + recvs[way][j - SUBS].astype(F32)
             sends[way][j] = value.astype(BF16)
             send_red(way, j)
+        if j >= 1 and len(chores) > 1:
+            chore()
+            if len(chores) > 1:
+                chore()
+        elif j == MESSAGES - 1:
+            chore()
     expert_out(t)
-    for j in range(MESSAGES - SUBS, MESSAGES):
+    while chores:
+        chore()
+    pending.extend(later)
+    finish()
+
+    for position, offset in enumerate(RETURN_ORDER):
+        value = ybuf[t, rows_at(offset), :]
         for way in range(2):
+            j = MESSAGES - SUBS + position
             wait_recv(recvs[way].at[j], red_rsem.at[way, j])
-    results = []
-    for sub in range(SUBS):
-        value = ybuf[t, sub * SUB_ROWS : (sub + 1) * SUB_ROWS]
-        value = value + recvs[0][MESSAGES - SUBS + sub].astype(F32)
-        value = value + recvs[1][MESSAGES - 1 - sub].astype(F32)
-        results.append(value.astype(BF16))
-    result = jnp.concatenate(results, axis=0)
-
-    back = dot(pick_out[0], result[:, :WIDE]) + dot(pick_out[1], result[:, WIDE:])
-    ret_send[...] = back.astype(BF16)
-    exchange(ret_send, ret_recv, ret_ssem, ret_rsem)
+            value = value + recvs[way][j].astype(F32)
+        value = value.astype(BF16)
+        back = dot(pick_out[0], value[:, :WIDE]) + dot(pick_out[1], value[:, WIDE:])
+        rows = pl.ds(pl.multiple_of(group_at(offset) * GROUP_ROWS, GROUP_ROWS), GROUP_ROWS)
+        ret_send[rows, :] = back.astype(BF16)
+        send_group(ret_send, ret_recv, ret_ssem, ret_rsem.at[0], offset)
+    pending.append(lambda: wait_recv(blocks_of(ret_send, DP - 1), ret_ssem.at[0]))
+    keep_own(ret_send, ret_recv)
+    finish_pages()
+    for f in range(len(FAR)):
+        wait_recv(mix_recv.at[f], mix_rsem.at[f])
+    wait_recv(blocks_of(ret_recv, DP - 1), ret_rsem.at[0])
 
     returned = ret_recv[...]
     mixture = dot(gather_top, returned) + dot(gather_rest, returned)
     for h in range(2):
         features = slice(h * WIDE, (h + 1) * WIDE)
         total = state[:, features].astype(F32) + mixture[h * TOKENS : (h + 1) * TOKENS]
+        for f in range(len(FAR)):
+            total = total + mix_recv[f, :, features].astype(F32)
         for r in range(4):
             layer_out[r, :, features] = total[4 * r : 4 * r + 4].astype(BF16)
 
@@ -583,8 +722,17 @@
             pltpu.VMEM((2, TOKENS, WIDE), F32),
             pltpu.VMEM((1, 128), jnp.int32),
             pltpu.SMEM((1, 128), jnp.int32),
-            pltpu.VMEM((2, ROWS, DP * BLOCK), BF16),
-            pltpu.VMEM((2, DP * BLOCK, ROWS), BF16),
+            pltpu.VMEM((2, SUB_ROWS, GROUP_ROWS), BF16),
+            pltpu.VMEM((2, GROUP_ROWS, SUB_ROWS), BF16),
+            pltpu.VMEM((ROWS, PART), F32),
+            pltpu.VMEM((TOKENS, PART), BF16),
+            pltpu.VMEM((len(FAR), TOKENS, PART), BF16),
+            pltpu.VMEM((len(FAR), DP * BLOCK, WIDE), BF16),
+            pltpu.VMEM((len(FAR), DP * BLOCK, WIDE), BF16),
+            pltpu.VMEM((len(FAR), DP * BLOCK, WIDE), BF16),
+            pltpu.VMEM((len(FAR), DP * BLOCK, WIDE), BF16),
+            pltpu.VMEM((len(FAR), TOKENS, PART), BF16),
+            pltpu.VMEM((len(FAR), TOKENS, PART), BF16),
             pltpu.VMEM((65, 16, WIDE), BF16),
             pltpu.VMEM((65, 16, WIDE), BF16),
             pltpu.VMEM((128, 16, WIDE), BF16),
@@ -614,11 +762,11 @@
             dma((17,)),
             dma((2,)), dma((2,)),
             dma((TP,)), dma((TP,)), dma((TP,)), dma((TP,)),
-            dma((1,)), dma((1,)),
+            dma((1,)), dma((4,)),
             dma((TP,)), dma((TP,)),
             dma((2, MESSAGES)), dma((2, MESSAGES)), dma((2, MESSAGES)), dma((2, MESSAGES)),
             dma((1,)), dma((1,)),
-        ],
+        ] + [dma((len(FAR),))] * 8,
         compiler_params=pltpu.CompilerParams(
             collective_id=0, has_side_effects=True, vmem_limit_bytes=60 * 1024 * 1024
         ),

time: 77.8 us -> 71.1 us (0.914)
  Pallas kernels: 77 us -> 70.3 us
    pallas_call x1, Pallas kernels: 74.5 us -> 67.9 us  [layer(): pl.pallas_call(layer_kernel, out_shape=(jax.ShapeDtypeStruct((128, 16, WI...]
where the time goes in v3:
time: 71.1 us; the launch traced here: 70.9 us
  Pallas kernels  70.3 us (99%)
    pallas_call x1, Pallas kernels, layer(): pl.pallas_call(layer_kernel, out_shape=(jax.ShapeDtypeStruct((128, 16, WI...  67.9 us
    pallas_call x1, Pallas kernels, place(): pl.pallas_call(place_kernel, out_shape=tuple((jax.ShapeDtypeStruct(a.shap...  2.43 us

profile of v3, /device:TPU:1, one launch (start us, length us, event | category | flops | bytes accessed | tf_op | source)
XLA Modules:
  0.0 70.9 jit_solution(6298386125365958229)
XLA Ops:
  0.6 67.9 %shard_map.166 = (bf16[128,16,256]{2,1,0:T(8,128)(2,1)}, bf16[128,16,256]{2,1,0:T(8,128)(2,1)}, bf16[4,4,512]{2,1,0:T(4,128)(2,1)}) custom-call(s32[4]{0:T(128)} %lengths.1, s32[1,64]{1,0:T(1,128)} %bitcast.13, bf16[4,4,4096]{2,1,0:T(4,128)(2,1)} %queries_in.1, bf16[4,4,256]{2,1,0:T(4,128)(2,1)} %new_keys_in.1, bf16[4,4,256]{2,1,0:T(4,128)(2,1)} %new_values_in.1, ...), custom_call_target="tpu_custom_call" | custom-call | tf_op jit(solution)/shard_map/pallas_call | solution.py:702
  68.5 2.4 %shard_map.167 = (bf16[128,16,256]{2,1,0:T(8,128)(2,1)}, bf16[128,16,256]{2,1,0:T(8,128)(2,1)}, bf16[4,4,512]{2,1,0:T(4,128)(2,1)}) custom-call(bf16[128,16,256]{2,1,0:T(8,128)(2,1)} %get-tuple-element.6.keys, bf16[128,16,256]{2,1,0:T(8,128)(2,1)} %get-tuple-element.7.values, bf16[4,4,512]{2,1,0:T(4,128)(2,1)} %get-tuple-element.8.rows), custom_call_target="tpu_custom_call" | custom-call | tf_op jit(solution)/shard_map/pallas_call | solution.py:799

commit v4 on v3

--- a/solution.py
+++ b/solution.py
@@ -103,15 +103,14 @@
 
     barrier = pltpu.get_barrier_semaphore()
 
-    @pl.loop(1, DP)
-    def _(d):
-        pl.semaphore_signal(
-            barrier, inc=1, device_id=(lax.rem(me + d, DP), t), device_id_type=MESH
-        )
-
     for d in range(1, TP):
         pl.semaphore_signal(
             barrier, inc=1, device_id=(me, lax.rem(t + d, TP)), device_id_type=MESH
+        )
+
+    for d in range(1, DP):
+        pl.semaphore_signal(
+            barrier, inc=1, device_id=(lax.rem(me + d, DP), t), device_id_type=MESH
         )
 
     kbuf[64] = jnp.zeros((16, WIDE), BF16)
@@ -128,6 +127,18 @@
     rows_together(new_values, new_rows.at[1])
     residual_rows = rows_together(residual, idrows)
     rows_together(queries, qrows)
+
+    dest = jnp.broadcast_to(page_dest[...], (64, 64))
+    page_row = iota((64, 64), 0)
+    page_col = iota((64, 64), 1)
+    dest_of = jnp.sum(jnp.where(page_row == page_col, dest, 0), axis=1, keepdims=True)
+    earlier = (dest == dest_of) & (page_col < page_row)
+    within = jnp.sum(jnp.where(earlier, 1, 0), axis=1, keepdims=True)
+    hit = dest_of * 4 + within == iota((64, 128), 1)
+    number = iota((64, 128), 0) - 64
+    inverse_row[...] = 64 + jnp.sum(jnp.where(hit, number, 0), axis=0, keepdims=True)
+    to_scalars = local(inverse_row, inverse, 16)
+    to_scalars.start()
 
     loads[0].wait()
     loads[1].wait()
@@ -228,21 +239,9 @@
     pending.append(finish_parts)
     part_recv[t] = part_send[t]
 
-    dest = jnp.broadcast_to(page_dest[...], (64, 64))
-    page_row = iota((64, 64), 0)
-    page_col = iota((64, 64), 1)
-    dest_of = jnp.sum(jnp.where(page_row == page_col, dest, 0), axis=1, keepdims=True)
-    earlier = (dest == dest_of) & (page_col < page_row)
-    within = jnp.sum(jnp.where(earlier, 1, 0), axis=1, keepdims=True)
-    hit = dest_of * 4 + within == iota((64, 128), 1)
-    number = iota((64, 128), 0) - 64
-    inverse_row[...] = 64 + jnp.sum(jnp.where(hit, number, 0), axis=0, keepdims=True)
-    to_scalars = local(inverse_row, inverse, 16)
-    to_scalars.start()
-
     to_scalars.wait()
 
-    @pl.loop(0, 128)
+    @pl.loop(0, 128, unroll=8)
     def _(slot):
         page = jnp.clip(inverse[0, slot], 0, 64)
         ksend[slot] = kbuf[page]
@@ -660,7 +659,6 @@
     while chores:
         chore()
     pending.extend(later)
-    finish()
 
     for position, offset in enumerate(RETURN_ORDER):
         value = ybuf[t, rows_at(offset), :]
@@ -673,8 +671,9 @@
         rows = pl.ds(pl.multiple_of(group_at(offset) * GROUP_ROWS, GROUP_ROWS), GROUP_ROWS)
         ret_send[rows, :] = back.astype(BF16)
         send_group(ret_send, ret_recv, ret_ssem, ret_rsem.at[0], offset)
+    keep_own(ret_send, ret_recv)
+    finish()
     pending.append(lambda: wait_recv(blocks_of(ret_send, DP - 1), ret_ssem.at[0]))
-    keep_own(ret_send, ret_recv)
     finish_pages()
     for f in range(len(FAR)):
         wait_recv(mix_recv.at[f], mix_rsem.at[f])

time: 71.1 us -> 70.6 us (level)
  no operation moved by 1% of the time
where the time goes in v4:
time: 70.6 us; the launch traced here: 70.4 us
  Pallas kernels  69.7 us (99%)
    pallas_call x1, Pallas kernels, layer(): pl.pallas_call(layer_kernel, out_shape=(jax.ShapeDtypeStruct((128, 16, WI...  67.3 us
    pallas_call x1, Pallas kernels, place(): pl.pallas_call(place_kernel, out_shape=tuple((jax.ShapeDtypeStruct(a.shap...  2.43 us

profile of v4, /device:TPU:1, one launch (start us, length us, event | category | flops | bytes accessed | tf_op | source)
XLA Modules:
  0.0 70.4 jit_solution(4017267135018063751)
XLA Ops:
  0.6 67.3 %shard_map.166 = (bf16[128,16,256]{2,1,0:T(8,128)(2,1)}, bf16[128,16,256]{2,1,0:T(8,128)(2,1)}, bf16[4,4,512]{2,1,0:T(4,128)(2,1)}) custom-call(s32[4]{0:T(128)} %lengths.1, s32[1,64]{1,0:T(1,128)} %bitcast.13, bf16[4,4,4096]{2,1,0:T(4,128)(2,1)} %queries_in.1, bf16[4,4,256]{2,1,0:T(4,128)(2,1)} %new_keys_in.1, bf16[4,4,256]{2,1,0:T(4,128)(2,1)} %new_values_in.1, ...), custom_call_target="tpu_custom_call" | custom-call | tf_op jit(solution)/shard_map/pallas_call | solution.py:701
  68.0 2.4 %shard_map.167 = (bf16[128,16,256]{2,1,0:T(8,128)(2,1)}, bf16[128,16,256]{2,1,0:T(8,128)(2,1)}, bf16[4,4,512]{2,1,0:T(4,128)(2,1)}) custom-call(bf16[128,16,256]{2,1,0:T(8,128)(2,1)} %get-tuple-element.6.keys, bf16[128,16,256]{2,1,0:T(8,128)(2,1)} %get-tuple-element.7.values, bf16[4,4,512]{2,1,0:T(4,128)(2,1)} %get-tuple-element.8.rows), custom_call_target="tpu_custom_call" | custom-call | tf_op jit(solution)/shard_map/pallas_call | solution.py:798
